TPU v7x, 512 devices: a whole 4x4x16 slice. The times are simulated.
512 devices in a mesh: dp: 32 (over z, x_lo), seq: 16 (over x_hi, y, core).
Axes of the slice: x: 4 (x_hi: 2, x_lo: 2; x = x_hi * 2 + x_lo), y: 4, z: 16, core: 2. Of those that a mesh axis runs over, the one named last changes fastest.
Arguments:
- image_projected: bfloat16 [32, 2048, 3, 2048], P('dp', 'seq'), may hold values from -8 to 8
- text_projected: bfloat16 [32, 512, 3, 2048], P('dp', 'seq'), may hold values from -8 to 8
- image_stream: bfloat16 [32, 2048, 3072], P('dp', 'seq'), may hold values from -3 to 3
- latents: float32 [32, 2048, 64], P('dp', 'seq'), may hold values from -6 to 6
- timesteps: int32 [32], P('dp'), may hold values from 0 to 9
- prompts: int32 [32], P('dp'), may hold values from 0 to 63
- noise_seeds: int32 [32], P('dp'), may hold values from 0 to 99999
- time_gate: bfloat16 [10, 3072], replicated, may hold values from -3 to 3
- prompt_gate: bfloat16 [64, 3072], replicated, may hold values from -3 to 3
- final_weight: bfloat16 [3072, 64], replicated, may hold values from -0.109375 to 0.109375
- saved_attention: bfloat16 [8192, 2048], P('dp'), may hold values from -6 to 6
- output_cotangent: bfloat16 [8192, 3072], P('dp', 'seq'), may hold values from -0.15625 to 0.15625
- master_weight: float32 [2048, 3072], P('dp', 'seq'), may hold values from -0.125 to 0.125
- first_moment: float32 [2048, 3072], P('dp', 'seq'), may hold values from -1.5 to 1.5
- second_moment: float32 [2048, 3072], P('dp', 'seq'), may hold values from 0.001 to 1
- average_weight: float32 [2048, 3072], P('dp', 'seq'), may hold values from -0.125 to 0.125
Outputs:
- velocity: float32 [32, 2048, 64], P('dp', 'seq')
- new_latents: float32 [32, 2048, 64], P('dp', 'seq')
- new_master: float32 [2048, 3072], P('dp', 'seq')
- new_first: float32 [2048, 3072], P('dp', 'seq')
- new_second: float32 [2048, 3072], P('dp', 'seq')
- new_average: float32 [2048, 3072], P('dp', 'seq')
All inputs are finite; a program needn't handle non-finite values.
Results may differ from a plain program's by a relative error of at most 0.025.
Values may be sent and summed in bfloat16 or wider, within the bound.
No kernel may reach another device: no remote copies, remote signals or barrier semaphores. Data moves between devices by JAX's collectives and lax.ppermute only.
A program may use at most 64 MiB of HBM per device.

v0:
```python
import math

import jax
import jax.numpy as jnp
from jax import lax
from jax.sharding import PartitionSpec as P

HEAD_DIM = 128
STEPS = 10
STEP_COUNT = 100


beta_first = 0.9
beta_second = 0.999
adam_epsilon = 1e-08
learn_rate = 0.0001
average_decay = 0.99
noise_level = 0.7
norm_epsilon = 1e-06


def hashed_noise(seed_value, token_index, channel_index):
    mixed_bits = seed_value * 73856093 + token_index * 19349663 + channel_index * 83492791
    mixed_bits = mixed_bits ^ jnp.right_shift(mixed_bits, 13)
    mixed_bits = mixed_bits * 1274126177
    mixed_bits = mixed_bits ^ jnp.right_shift(mixed_bits, 16)
    low_bits = mixed_bits & 65535
    return ((low_bits.astype(jnp.float32) + 0.5) / 32768.0 - 1.0) * math.sqrt(3.0)


def attend(queries, keys, values):
    query_count = queries.shape[0]
    score_scale = queries.shape[-1] ** (-0.5)
    block_rows = 512
    while query_count % block_rows:
        block_rows = block_rows // 2
    grouped = queries.reshape(
        query_count // block_rows, block_rows, queries.shape[1], queries.shape[2]
    )

    def one_block(query_block):
        scores = (
            jnp.einsum("qhd,khd->hqk", query_block, keys, preferred_element_type=jnp.float32)
            * score_scale
        )
        peak_score = jnp.max(scores, axis=-1, keepdims=True)
        expo = jnp.exp(scores - peak_score)
        denominator = jnp.sum(expo, axis=-1)
        mixed = jnp.einsum(
            "hqk,khd->qhd", expo.astype(jnp.bfloat16), values, preferred_element_type=jnp.float32
        )
        return (mixed / jnp.transpose(denominator)[:, :, None]).astype(jnp.bfloat16)

    return lax.map(one_block, grouped).reshape(query_count, queries.shape[1], queries.shape[2])


def local(
    image_projected,
    text_projected,
    image_stream,
    latents,
    timesteps,
    prompts,
    noise_seeds,
    time_gate,
    prompt_gate,
    final_weight,
    saved_attention,
    output_cotangent,
    master_weight,
    first_moment,
    second_moment,
    average_weight,
):
    gradient = lax.psum_scatter(
        lax.dot_general(
            saved_attention,
            output_cotangent,
            (((0,), (0,)), ((), ())),
            preferred_element_type=jnp.float32,
        ).astype(jnp.bfloat16),
        "dp",
        scatter_dimension=0,
        tiled=True,
    ).astype(jnp.float32)
    new_first = beta_first * first_moment + (1.0 - beta_first) * gradient
    new_second = beta_second * second_moment + (1.0 - beta_second) * gradient * gradient
    first_corr = 1.0 - beta_first**STEP_COUNT
    second_corr = 1.0 - beta_second**STEP_COUNT
    new_master = master_weight - learn_rate * (new_first / first_corr) / (
        jnp.sqrt(new_second / second_corr) + adam_epsilon
    )
    new_average = average_decay * average_weight + (1.0 - average_decay) * new_master
    sampler_weight = average_weight.astype(jnp.bfloat16)
    image_local = image_projected[0]
    text_local = text_projected[0]
    image_tokens = image_local.shape[0]
    width_att = image_local.shape[2]
    head_count = width_att // HEAD_DIM
    image_split = image_local.reshape(image_tokens, 3, head_count, HEAD_DIM)
    text_split = text_local.reshape(text_local.shape[0], 3, head_count, HEAD_DIM)
    image_heads, text_heads = (
        lax.all_to_all(image_split, "seq", split_axis=2, concat_axis=0, tiled=True),
        lax.all_to_all(text_split, "seq", split_axis=2, concat_axis=0, tiled=True),
    )
    keys = jnp.concatenate([image_heads[:, 1], text_heads[:, 1]], 0)
    values = jnp.concatenate([image_heads[:, 2], text_heads[:, 2]], 0)
    heads_out = attend(image_heads[:, 0], keys, values)
    stream = image_stream[0]
    token_heads = lax.all_to_all(heads_out, "seq", split_axis=0, concat_axis=1, tiled=True)
    attention_flat = token_heads.reshape(image_tokens, width_att)
    column_slab = lax.all_gather(sampler_weight, "dp", axis=0, tiled=True)
    branch = jnp.dot(
        attention_flat,
        lax.all_gather(column_slab, "seq", axis=1, tiled=True),
        preferred_element_type=jnp.float32,
    )
    step_index = timesteps[0]
    prompt_index = prompts[0]
    step_table = jnp.arange(time_gate.shape[0], dtype=jnp.int32)[:, None]
    prompt_table = jnp.arange(prompt_gate.shape[0], dtype=jnp.int32)[:, None]
    gate = jnp.sum(jnp.where(step_table == step_index, time_gate.astype(jnp.float32), 0.0), 0)
    gate = gate + jnp.sum(
        jnp.where(prompt_table == prompt_index, prompt_gate.astype(jnp.float32), 0.0), 0
    )
    hidden = stream.astype(jnp.float32) + gate[None, :] * branch
    mean_value = jnp.mean(hidden, axis=-1, keepdims=True)
    centered = hidden - mean_value
    variance = jnp.mean(centered * centered, axis=-1, keepdims=True)
    normalized = (centered / jnp.sqrt(variance + norm_epsilon)).astype(jnp.bfloat16)
    velocity = jnp.dot(normalized, final_weight, preferred_element_type=jnp.float32)
    latent_now = latents[0]
    step_float = step_index.astype(jnp.float32)
    time_now = 1.0 - (step_float + 1.0) / (STEPS + 2.0)
    time_next = 1.0 - (step_float + 2.0) / (STEPS + 2.0)
    sigma = noise_level * jnp.sqrt(time_now / (1.0 - time_now))
    token_index = (
        lax.axis_index("seq") * image_tokens + jnp.arange(image_tokens, dtype=jnp.int32)[:, None]
    )
    channel_index = jnp.arange(latent_now.shape[1], dtype=jnp.int32)[None, :]
    noise = hashed_noise(noise_seeds[0], token_index, channel_index)
    drift = velocity + sigma * sigma / (2.0 * time_now) * (latent_now + (1.0 - time_now) * velocity)
    stepped = (
        latent_now + drift * (time_next - time_now) + sigma * jnp.sqrt(time_now - time_next) * noise
    )
    return (velocity[None], stepped[None], new_master, new_first, new_second, new_average)


def solution(mesh):
    in_specs = (
        P("dp", "seq", None, None),
        P("dp", "seq", None, None),
        P("dp", "seq", None),
        P("dp", "seq", None),
        P("dp"),
        P("dp"),
        P("dp"),
        P(),
        P(),
        P(),
        P("dp", None),
        P("dp", "seq"),
        P("dp", "seq"),
        P("dp", "seq"),
        P("dp", "seq"),
        P("dp", "seq"),
    )
    out_specs = (
        P("dp", "seq", None),
        P("dp", "seq", None),
        P("dp", "seq"),
        P("dp", "seq"),
        P("dp", "seq"),
        P("dp", "seq"),
    )
    return jax.shard_map(local, mesh=mesh, in_specs=in_specs, out_specs=out_specs, check_vma=False)
```

profile of v0, /device:TPU:1, one launch (start us, length us, event | category | flops | bytes accessed | tf_op | source)
XLA Modules:
  0.0 364.7 jit_solution(17328925410482901802)
XLA Ops:
  7.2 0.0 copy-start
  7.2 0.0 copy-start.6
  7.2 0.0 copy-start.7
  7.2 0.0 copy-start.8
  7.2 0.0 copy-start.5
  7.2 0.0 reduce-scatter.2.cloned.1.call-start
  7.3 1.1 copy-done
  8.4 2.4 convolution_convert_fusion
  10.8 0.0 reduce-scatter.2.cloned.1.call-update
  10.8 0.0 all-gather.2.cloned.1.call-start
  10.8 118.0 %reduce-scatter.2.cloned.1.call-done = bf16[64,192]{1,0:T(8,128)(2,1)} async-done(((bf16[2048,192]{1,0:T(8,128)(2,1)}), bf16[64,192]{1,0:T(8,128)(2,1)}) %reduce-scatter.2.cloned.1.call-update) | async-done | bytes 24592 | tf_op jit(solution)/shard_map/reduce_scatter | solution.py:75
  128.8 0.0 copy-done.6
  128.8 0.0 copy-done.7
  128.8 0.0 copy-done.8
  128.8 0.0 copy-done.5
  128.8 1.5 multiply_add_fusion
  130.3 53.0 %all_gather.6 = bf16[2048,192]{1,0:T(8,128)(2,1)S(1)} all-gather(bf16[64,192]{1,0:T(8,128)(2,1)S(1)} %get-tuple-element.85), channel_id=1, replica_groups=mesh['dp'=32,'seq'=16] {'dp'}, dimensions={0}, use_global_device_ids=true | all-gather | bytes 811008 | tf_op jit(solution)/shard_map/all_gather | solution.py:112
  183.3 1.2 copy.54
  184.5 0.0 all-gather.2.cloned.1.call-update
  184.6 0.0 copy-done.2
  184.6 0.1 copy.56
  184.7 0.9 copy.49
  185.5 42.8 %all-to-all-start.1 = ((bf16[32,3,16,128]{3,0,1,2:T(8,128)(2,1)}), bf16[32,3,16,128]{3,0,1,2:T(8,128)(2,1)S(1)}, u32[]{:S(2)}, u32[]{:S(2)}) async-start(bf16[32,3,16,128]{3,0,1,2:T(8,128)(2,1)} %copy.49), calls=%async_computation.1 | async-start | bytes 786432 | tf_op jit(solution)/shard_map/all_to_all | solution.py:104
  228.3 1.9 copy.46
  230.2 1.6 copy.47
  231.8 6.4 %all-to-all-done.1 = bf16[32,3,16,128]{3,0,1,2:T(8,128)(2,1)S(1)} async-done(((bf16[32,3,16,128]{3,0,1,2:T(8,128)(2,1)}), bf16[32,3,16,128]{3,0,1,2:T(8,128)(2,1)S(1)}, u32[]{:S(2)}, u32[]{:S(2)}) %all-to-all-start.1) | async-done | bytes 393248 | tf_op jit(solution)/shard_map/all_to_all | solution.py:104
  238.2 4.7 %all-to-all-start = ((bf16[128,3,16,128]{3,0,1,2:T(8,128)(2,1)}), bf16[128,3,16,128]{3,0,1,2:T(8,128)(2,1)S(1)}, u32[]{:S(2)}, u32[]{:S(2)}) async-start(bf16[128,3,16,128]{3,0,1,2:T(8,128)(2,1)} %copy.47), calls=%async_computation | async-start | bytes 3145728 | tf_op jit(solution)/shard_map/all_to_all | solution.py:103
  244.3 25.7 %all-to-all-done = bf16[128,3,16,128]{3,0,1,2:T(8,128)(2,1)S(1)} async-done(((bf16[128,3,16,128]{3,0,1,2:T(8,128)(2,1)}), bf16[128,3,16,128]{3,0,1,2:T(8,128)(2,1)S(1)}, u32[]{:S(2)}, u32[]{:S(2)}) %all-to-all-start) | async-done | bytes 1572896 | tf_op jit(solution)/shard_map/all_to_all | solution.py:103
  269.9 0.2 copy.48
  270.1 0.1 slice_bitcast_fusion
  270.2 0.1 pad_maximum_fusion
  270.3 13.3 %while.10 = (s32[]{:T(128)}, bf16[4,512,1,128]{3,1,2,0:T(8,128)(2,1)}, bf16[4,512,1,128]{3,1,2,0:T(8,128)(2,1)S(1)}, bf16[2560,1,128]{2,0,1:T(8,128)(2,1)S(1)}, bf16[2560,1,128]{2,0,1:T(8,128)(2,1)S(1)}, /*index=5*/s32[]{:T(128)}) while((s32[]{:T(128)}, bf16[4,512,1,128]{3,1,2,0:T(8,128)(2,1)}, bf16[4,512,1,128]{3,1,2,0:T(8,128)(2,1)S(1)}, ...), condition=%wide.region_5.6_spmd, body=%wide.region_2.5_spmd.sunk | while | flops 679083008 | bytes 17312328 | solution.py:54
  270.3 0.9 fusion.57
  271.3 0.8 fusion.58
  272.1 1.6 fusion.59
  273.7 0.9 fusion.57
  274.6 0.8 fusion.58
  275.4 1.6 fusion.59
  277.0 0.9 fusion.57
  277.9 0.8 fusion.58
  278.8 1.6 fusion.59
  280.3 0.9 fusion.57
  281.3 0.8 fusion.58
  282.1 1.6 fusion.59
  283.7 0.5 broadcast.74
  284.2 2.1 reduce.4
  286.3 0.9 reshape.95
  287.3 7.8 %all-to-all-start.2 = ((bf16[16,2,8192]{2,1,0:T(2,128)(2,1)}), bf16[16,2,8192]{2,1,0:T(2,128)(2,1)S(1)}, u32[]{:S(2)}, u32[]{:S(2)}) async-start(bf16[16,2,8192]{2,1,0:T(2,128)(2,1)} %reshape.95), calls=%async_computation.2 | async-start | bytes 1048576 | tf_op jit(solution)/shard_map/all_to_all | solution.py:110
  295.9 0.0 copy-done.4
  295.9 0.1 select_reduce_fusion.1
  296.0 0.2 select_reduce_fusion
  296.3 16.3 %all-to-all-done.2 = bf16[16,2,8192]{2,1,0:T(2,128)(2,1)S(1)} async-done(((bf16[16,2,8192]{2,1,0:T(2,128)(2,1)}), bf16[16,2,8192]{2,1,0:T(2,128)(2,1)S(1)}, u32[]{:S(2)}, u32[]{:S(2)}) %all-to-all-start.2) | async-done | bytes 524320 | tf_op jit(solution)/shard_map/all_to_all | solution.py:110
  312.6 0.5 reshape.96
  313.1 0.1 copy.55
  313.2 0.0 copy-start.1
  313.2 0.3 copy.53
  313.5 33.1 %all-gather.2.cloned.1.call-done = bf16[2048,3072]{0,1:T(8,128)(2,1)} async-done(((bf16[2048,192]{0,1:T(8,128)(2,1)}), bf16[2048,3072]{0,1:T(8,128)(2,1)}) %all-gather.2.cloned.1.call-update) | async-done | bytes 12582928 | tf_op jit(solution)/shard_map/all_gather | solution.py:115
  346.5 8.9 %fusion.44 = (f32[128]{0:T(128)S(1)}, f32[128,3072]{1,0:T(8,128)S(1)}) fusion(bf16[128,2048]{0,1:T(8,128)(2,1)S(1)} %bitcast.107, bf16[2048,3072]{0,1:T(8,128)(2,1)} %all-gather.2.cloned.1.call-done, f32[3072]{0:T(1024)S(1)} %add.101, bf16[1,128,3072]{2,1,0:T(8,128)(2,1)S(1)} %copy-done.1), kind=kOutput, calls=%fused_computation.59 | convolution fusion | flops 1612185472 | bytes 15479296 | tf_op jit(solution)/shard_map/dot_general | solution.py:113
  355.4 0.0 copy-start.11
  355.5 0.3 multiply_reduce_fusion
  355.8 0.7 copy-done.11
  356.4 0.5 fusion.26
  356.9 0.3 copy-done.9
  357.2 0.7 fusion.37
  (18 shorter events, 0.1 us)
Async XLA Ops:
  7.2 1.2 copy-start
  7.2 121.6 %copy-start.6 = (f32[64,192]{1,0:T(8,128)S(1)}, f32[64,192]{1,0:T(8,128)}, u32[]{:S(2)}) copy-start(f32[64,192]{1,0:T(8,128)} %param.30) | copy-start | bytes 147460
  7.2 121.6 %copy-start.7 = (f32[64,192]{1,0:T(8,128)S(1)}, f32[64,192]{1,0:T(8,128)}, u32[]{:S(2)}) copy-start(f32[64,192]{1,0:T(8,128)} %param.31) | copy-start | bytes 147460
  7.2 121.6 %copy-start.8 = (f32[64,192]{1,0:T(8,128)S(1)}, f32[64,192]{1,0:T(8,128)}, u32[]{:S(2)}) copy-start(f32[64,192]{1,0:T(8,128)} %param.32) | copy-start | bytes 147460
  7.2 121.6 %copy-start.5 = (f32[64,192]{1,0:T(8,128)S(1)}, f32[64,192]{1,0:T(8,128)}, u32[]{:S(2)}) copy-start(f32[64,192]{1,0:T(8,128)} %param.33) | copy-start | bytes 147460
  7.2 121.6 %reduce-scatter.2.cloned.1.call-start = ((), (), s32[]{:S(2)}) async-start(), calls=%async_computation.5 | async-start | bytes 1081344 | tf_op jit(solution)/shard_map/reduce_scatter | solution.py:75
  10.8 335.8 %all-gather.2.cloned.1.call-start = ((), (), s32[]{:S(2)}) async-start(), calls=%async_computation.4 | async-start | bytes 13369344 | tf_op jit(solution)/shard_map/all_gather | solution.py:115
  183.3 1.3 copy-start.2
  185.5 52.7 %all-to-all-start.1 = ((bf16[32,3,16,128]{3,0,1,2:T(8,128)(2,1)}), bf16[32,3,16,128]{3,0,1,2:T(8,128)(2,1)S(1)}, u32[]{:S(2)}, u32[]{:S(2)}) async-start(bf16[32,3,16,128]{3,0,1,2:T(8,128)(2,1)} %copy.49), calls=%async_computation.1 | async-start | bytes 786432 | tf_op jit(solution)/shard_map/all_to_all | solution.py:104
  238.2 31.7 %all-to-all-start = ((bf16[128,3,16,128]{3,0,1,2:T(8,128)(2,1)}), bf16[128,3,16,128]{3,0,1,2:T(8,128)(2,1)S(1)}, u32[]{:S(2)}, u32[]{:S(2)}) async-start(bf16[128,3,16,128]{3,0,1,2:T(8,128)(2,1)} %copy.47), calls=%async_computation | async-start | bytes 3145728 | tf_op jit(solution)/shard_map/all_to_all | solution.py:103
  284.2 11.7 %copy-start.4 = (bf16[10,3072]{1,0:T(8,128)(2,1)S(1)}, bf16[10,3072]{1,0:T(8,128)(2,1)}, u32[]{:S(2)}) copy-start(bf16[10,3072]{1,0:T(8,128)(2,1)} %param.25) | copy-start | bytes 184324
  284.2 11.8 %copy-start.3 = (bf16[64,3072]{1,0:T(8,128)(2,1)S(1)}, bf16[64,3072]{1,0:T(8,128)(2,1)}, u32[]{:S(2)}) copy-start(bf16[64,3072]{1,0:T(8,128)(2,1)} %param.26) | copy-start | bytes 1179652
  287.3 25.3 %all-to-all-start.2 = ((bf16[16,2,8192]{2,1,0:T(2,128)(2,1)}), bf16[16,2,8192]{2,1,0:T(2,128)(2,1)S(1)}, u32[]{:S(2)}, u32[]{:S(2)}) async-start(bf16[16,2,8192]{2,1,0:T(2,128)(2,1)} %reshape.95), calls=%async_computation.2 | async-start | bytes 1048576 | tf_op jit(solution)/shard_map/all_to_all | solution.py:110
  313.2 33.4 %copy-start.1 = (bf16[1,128,3072]{2,1,0:T(8,128)(2,1)S(1)}, bf16[1,128,3072]{2,1,0:T(8,128)(2,1)}, u32[]{:S(2)}) copy-start(bf16[1,128,3072]{2,1,0:T(8,128)(2,1)} %param.20) | copy-start | bytes 2359300
  355.4 1.0 copy-start.11
  356.4 0.8 copy-start.9
  357.2 0.7 copy-start.10
Sparse Core Ops, SparseCore 0:
  10.9 117.8 reduce-scatter.1
  184.7 161.7 all-gather.1
where the time goes:
time: 365 us
  waiting for transfers between devices  199 us (55%)
  starting transfers between devices  55.4 us (15%)
  blocking collectives  53 us (15%)
  matrix products  21.7 us (6%)
  between operations  16.4 us (4%)
  local copies, waits for them, and re-layouts  10.4 us (3%)
  other arithmetic  8.4 us (2%)
    reduce_scatter x1, waiting for transfers between devices, local(): lax.psum_scatter(lax.dot_general(saved_attention, output_cotangent, (((0,...  118 us
    all_gather x1, blocking collectives, local(): column_slab = lax.all_gather(sampler_weight, 'dp', axis=0, tiled=True)  53 us
    all_to_all x1, starting transfers between devices, local(): lax.all_to_all(text_split, 'seq', split_axis=2, concat_axis=0, tiled=True)  42.8 us
    all_gather x1, waiting for transfers between devices, local(): lax.all_gather(column_slab, 'seq', axis=1, tiled=True)  33.1 us
    all_to_all x1, waiting for transfers between devices, local(): lax.all_to_all(image_split, 'seq', split_axis=2, concat_axis=0, tiled=True)  25.7 us
    all_to_all x1, waiting for transfers between devices, local(): lax.all_to_all(heads_out, 'seq', split_axis=0, concat_axis=1, tiled=True)  16.3 us
    dot_general x1, matrix products, local(): jnp.dot(attention_flat, lax.all_gather(column_slab, 'seq', axis=1, tiled=...  8.9 us
    all_to_all x1, starting transfers between devices, local(): lax.all_to_all(heads_out, 'seq', split_axis=0, concat_axis=1, tiled=True)  7.85 us
  transfers between devices with their start and end apart: 5, of which 5 were waited for; matrix products, arithmetic and copies ran while one was open for 6% of the time, Pallas kernels for 0%

commit v1 on v0

v1 whole, which is shorter than its diff:
```python
import functools
import math

import jax
import jax.numpy as jnp
from jax import lax
from jax.experimental import pallas as pl
from jax.experimental.pallas import tpu as pltpu
from jax.sharding import PartitionSpec as P

HEAD_DIM = 128
STEPS = 10
STEP_COUNT = 100


beta_first = 0.9
beta_second = 0.999
adam_epsilon = 1e-08
learn_rate = 0.0001
average_decay = 0.99
noise_level = 0.7
norm_epsilon = 1e-06


def hashed_noise(seed_value, token_index, channel_index):
    mixed_bits = seed_value * 73856093 + token_index * 19349663 + channel_index * 83492791
    mixed_bits = mixed_bits ^ jnp.right_shift(mixed_bits, 13)
    mixed_bits = mixed_bits * 1274126177
    mixed_bits = mixed_bits ^ jnp.right_shift(mixed_bits, 16)
    low_bits = mixed_bits & 65535
    return ((low_bits.astype(jnp.float32) + 0.5) / 32768.0 - 1.0) * math.sqrt(3.0)


AXES = ("z", "xl", "xh", "y", "c")
DP = ("z", "xl")
SEQ = ("xh", "y", "c")
MEBI = 1024 * 1024
VMEM = pl.BlockSpec(memory_space=pltpu.VMEM)
SMEM = pl.BlockSpec(memory_space=pltpu.SMEM)


def pack_kernel(image_ref, text_ref, out_ref):
    heads, _, _, width = out_ref.shape
    image_tokens = image_ref.shape[1]
    for head in range(heads):
        span = slice(head * width, (head + 1) * width)
        out_ref[head, :, :image_tokens, :] = image_ref[:, :, span]
        out_ref[head, :, image_tokens:, :] = text_ref[:, :, span]


def pack(image, text):
    tokens = image.shape[1] + text.shape[1]
    return pl.pallas_call(
        pack_kernel,
        out_shape=jax.ShapeDtypeStruct((16, 3, tokens, HEAD_DIM), jnp.bfloat16),
        in_specs=[VMEM, VMEM],
        out_specs=VMEM,
        compiler_params=pltpu.CompilerParams(vmem_limit_bytes=16 * MEBI),
        name="pack",
    )(image, text)


def attention_kernel(packed_ref, out_ref, widened_ref):
    sources, _, tokens, width = packed_ref.shape
    image_tokens = out_ref.shape[2]
    scale = width ** (-0.5) * math.log2(math.e)
    keys = packed_ref[:, 1].reshape(sources * tokens, width)
    widened_ref[:, :width] = packed_ref[:, 2].reshape(sources * tokens, width)
    widened_ref[:, width:] = jnp.ones((sources * tokens, width), jnp.bfloat16)

    def step(index, carry):
        queries = packed_ref[pl.ds(index * 2, 2), 0, :image_tokens, :]
        queries = queries.reshape(2 * image_tokens, width)
        scores = lax.dot_general(
            queries, keys, (((1,), (1,)), ((), ())), preferred_element_type=jnp.float32
        )
        peak = jnp.max(scores, axis=-1, keepdims=True)
        expo = jnp.exp2((scores - peak) * scale)
        mixed = jnp.dot(
            expo.astype(jnp.bfloat16), widened_ref[...], preferred_element_type=jnp.float32
        )
        result = (mixed[:, :width] / mixed[:, width:]).astype(jnp.bfloat16)
        row = index % 4
        half = index // 4
        for core in range(2):
            block = result[core * image_tokens : (core + 1) * image_tokens]
            for target in range(4):
                out_ref[half * 8 + target * 2 + core, row] = block
        return carry

    lax.fori_loop(0, sources // 2, step, 0, unroll=2)


def attend(packed, image_tokens):
    sources, _, tokens, width = packed.shape
    return pl.pallas_call(
        attention_kernel,
        out_shape=jax.ShapeDtypeStruct((16, 4, image_tokens, HEAD_DIM), jnp.bfloat16),
        in_specs=[VMEM],
        out_specs=VMEM,
        scratch_shapes=[pltpu.VMEM((sources * tokens, 2 * width), jnp.bfloat16)],
        compiler_params=pltpu.CompilerParams(vmem_limit_bytes=24 * MEBI),
        cost_estimate=pl.CostEstimate(
            flops=2700000000, bytes_accessed=4000000, transcendentals=5300000
        ),
        name="attend",
    )(packed)


def project_kernel(heads_ref, weight_ref, out_ref, flat_ref):
    head_count, _, width = heads_ref.shape
    for head in range(head_count):
        flat_ref[:, head * width : (head + 1) * width] = heads_ref[head]
    out_ref[...] = jnp.dot(
        flat_ref[...], weight_ref[...], preferred_element_type=jnp.float32
    ).astype(jnp.bfloat16)


def project(heads, weight):
    head_count, tokens, width = heads.shape
    return pl.pallas_call(
        project_kernel,
        out_shape=jax.ShapeDtypeStruct((tokens, weight.shape[1]), jnp.bfloat16),
        in_specs=[VMEM, VMEM],
        out_specs=VMEM,
        scratch_shapes=[pltpu.VMEM((tokens, head_count * width), jnp.bfloat16)],
        compiler_params=pltpu.CompilerParams(vmem_limit_bytes=24 * MEBI),
        cost_estimate=pl.CostEstimate(
            flops=1600000000, bytes_accessed=6000000, transcendentals=0
        ),
        name="project",
    )(heads, weight)


def finish_kernel(
    slope_ref, branch_ref, stream_ref, gate_ref, final_ref, base_ref, velocity_ref, stepped_ref, hidden_ref
):
    quarters, _, columns = branch_ref.shape
    half = columns // 2
    features = stream_ref.shape[1]
    total = 0.0
    for far in range(2):
        for quarter in range(quarters):
            start = far * quarters * half + quarter * half
            span = slice(start, start + half)
            part = branch_ref[quarter, :, far * half : (far + 1) * half].astype(jnp.float32)
            hidden = stream_ref[:, span].astype(jnp.float32) + gate_ref[:, span] * part
            hidden_ref[:, span] = hidden
            total = total + jnp.sum(hidden, axis=-1, keepdims=True)
    centered = hidden_ref[...] - total / features
    variance = jnp.sum(centered * centered, axis=-1, keepdims=True) / features
    normalized = (centered * lax.rsqrt(variance + norm_epsilon)).astype(jnp.bfloat16)
    velocity = lax.dot_general(
        final_ref[...],
        normalized,
        (((1,), (1,)), ((), ())),
        preferred_element_type=jnp.float32,
    )
    velocity_ref[...] = velocity
    stepped_ref[...] = base_ref[...] + slope_ref[0] * velocity


def finish(slope, branch, stream, gate, final, base):
    shape = jax.ShapeDtypeStruct(base.shape, jnp.float32)
    return pl.pallas_call(
        finish_kernel,
        out_shape=(shape, shape),
        in_specs=[SMEM, VMEM, VMEM, VMEM, VMEM, VMEM],
        out_specs=(VMEM, VMEM),
        scratch_shapes=[pltpu.VMEM(stream.shape, jnp.float32)],
        compiler_params=pltpu.CompilerParams(vmem_limit_bytes=16 * MEBI),
        name="finish",
    )(slope, branch, stream, gate, final, base)


def deal(bit, blocks, run, keep_ref, give_ref):
    pairs = blocks.reshape((blocks.shape[0] // (2 * run), 2, run) + blocks.shape[1:])
    even = pairs[:, 0].reshape(keep_ref.shape)
    odd = pairs[:, 1].reshape(keep_ref.shape)
    keep_ref[...] = jnp.where(bit == 0, even, odd)
    give_ref[...] = jnp.where(bit == 0, odd, even)


def partial_kernel(run, bit_ref, saved_ref, cotangent_ref, keep_ref, give_ref):
    partial = lax.dot_general(
        saved_ref[...],
        cotangent_ref[...],
        (((0,), (0,)), ((), ())),
        preferred_element_type=jnp.float32,
    ).astype(jnp.bfloat16)
    rows, columns = keep_ref.shape[1:]
    blocks = partial.reshape(partial.shape[0] // rows, rows, columns)
    deal(bit_ref[0], blocks, run, keep_ref, give_ref)


def merge_kernel(run, bit_ref, kept_ref, taken_ref, keep_ref, give_ref):
    total = kept_ref[...].astype(jnp.float32) + taken_ref[...].astype(jnp.float32)
    deal(bit_ref[0], total.astype(jnp.bfloat16), run, keep_ref, give_ref)


def split_call(kernel, run, bit, first, second, blocks, rows, columns, name):
    half = jax.ShapeDtypeStruct((blocks // 2, rows, columns), jnp.bfloat16)
    return pl.pallas_call(
        functools.partial(kernel, run),
        out_shape=(half, half),
        in_specs=[SMEM, VMEM, VMEM],
        out_specs=(VMEM, VMEM),
        compiler_params=pltpu.CompilerParams(vmem_limit_bytes=16 * MEBI),
        name=name,
    )(bit, first, second)


def axis_bit(axis, distance):
    return ((lax.axis_index(axis) // distance) % 2).astype(jnp.int32).reshape(1)


def exchange(value, axis, distance):
    size = lax.axis_size(axis)
    return lax.ppermute(value, axis, [(k, k ^ distance) for k in range(size)])


def beside(own, other, axis, dimension):
    first = lax.axis_index(axis) == 0
    return jnp.concatenate([jnp.where(first, own, other), jnp.where(first, other, own)], dimension)


def local(
    image_projected,
    text_projected,
    image_stream,
    latents,
    timesteps,
    prompts,
    noise_seeds,
    time_gate,
    prompt_gate,
    final_weight,
    saved_attention,
    output_cotangent,
    master_weight,
    first_moment,
    second_moment,
    average_weight,
):
    image_tokens = image_projected.shape[1]
    own_rows, own_columns = master_weight.shape

    packed = pack(image_projected[0].transpose(1, 0, 2), text_projected[0].transpose(1, 0, 2))

    def share(kernel, step, first, second):
        axis, distance, run = order[step]
        return split_call(
            kernel,
            run,
            axis_bit(axis, distance),
            first,
            second,
            32 >> step,
            own_rows,
            own_columns,
            kernel.__name__[:-7],
        )

    order = (("z", 1, 2), ("z", 2, 2), ("xl", 1, 1), ("z", 4, 1), ("z", 8, 1))
    keep, give = share(partial_kernel, 0, saved_attention, output_cotangent)
    taken = exchange(give, "z", 1)

    sampler_weight = lax.optimization_barrier(average_weight.astype(jnp.bfloat16))
    pieces = beside(sampler_weight, exchange(sampler_weight, "c", 1), "c", 1)
    pieces = beside(pieces, exchange(pieces, "xh", 1), "xh", 1)
    pieces = beside(pieces, exchange(pieces, "xl", 1), "xl", 0)
    pieces, taken, packed = lax.optimization_barrier((pieces, taken, packed))
    weight = lax.all_gather(pieces, "z", axis=0, tiled=True)

    arrived = lax.all_to_all(packed, SEQ, split_axis=0, concat_axis=0, tiled=True)
    for step in range(1, len(order)):
        keep, give = share(merge_kernel, step, keep, taken)
        if step == 3:
            keep, give, arrived = lax.optimization_barrier((keep, give, arrived))
        taken = exchange(give, *order[step][:2])

    heads_out = attend(arrived, image_tokens)
    heads = lax.all_to_all(heads_out, SEQ, split_axis=0, concat_axis=0, tiled=True)
    heads, keep, taken = lax.optimization_barrier((heads, keep, taken))
    heads = heads.reshape(16, 4 * image_tokens, HEAD_DIM)

    gradient = keep[0].astype(jnp.float32) + taken[0].astype(jnp.float32)
    new_first = beta_first * first_moment + (1.0 - beta_first) * gradient
    new_second = beta_second * second_moment + (1.0 - beta_second) * gradient * gradient
    first_corr = 1.0 - beta_first**STEP_COUNT
    second_corr = 1.0 - beta_second**STEP_COUNT
    new_master = master_weight - learn_rate * (new_first / first_corr) / (
        jnp.sqrt(new_second / second_corr) + adam_epsilon
    )
    new_average = average_decay * average_weight + (1.0 - average_decay) * new_master

    step_index = timesteps[0]
    prompt_index = prompts[0]
    step_table = jnp.arange(time_gate.shape[0], dtype=jnp.int32)[:, None]
    prompt_table = jnp.arange(prompt_gate.shape[0], dtype=jnp.int32)[:, None]
    gate = jnp.sum(
        jnp.where(step_table == step_index, time_gate.astype(jnp.float32), 0.0), 0, keepdims=True
    )
    gate = gate + jnp.sum(
        jnp.where(prompt_table == prompt_index, prompt_gate.astype(jnp.float32), 0.0),
        0,
        keepdims=True,
    )
    latent_now = latents[0].transpose(1, 0)
    step_float = step_index.astype(jnp.float32)
    time_now = 1.0 - (step_float + 1.0) / (STEPS + 2.0)
    time_next = 1.0 - (step_float + 2.0) / (STEPS + 2.0)
    sigma = noise_level * jnp.sqrt(time_now / (1.0 - time_now))
    token_index = (
        lax.axis_index(SEQ) * image_tokens + jnp.arange(image_tokens, dtype=jnp.int32)[None, :]
    )
    channel_index = jnp.arange(latent_now.shape[0], dtype=jnp.int32)[:, None]
    noise = hashed_noise(noise_seeds[0], token_index, channel_index)
    pull = sigma * sigma / (2.0 * time_now)
    span = time_next - time_now
    base = latent_now + pull * latent_now * span + sigma * jnp.sqrt(time_now - time_next) * noise
    slope = (span * (1.0 + pull * (1.0 - time_now))).reshape(1)

    branch = project(heads, weight)
    branch = branch.reshape(4, image_tokens, branch.shape[1])
    branch = lax.all_to_all(branch, "y", split_axis=0, concat_axis=0, tiled=True)
    velocity, stepped = finish(
        slope, branch, image_stream[0], gate, final_weight.transpose(1, 0), base
    )
    velocity = velocity.transpose(1, 0)
    stepped = stepped.transpose(1, 0)
    return (velocity[None], stepped[None], new_master, new_first, new_second, new_average)


def solution(mesh):
    fine = jax.sharding.Mesh(mesh.devices.reshape(16, 2, 2, 4, 2), AXES)
    in_specs = (
        P(DP, SEQ, None, None),
        P(DP, SEQ, None, None),
        P(DP, SEQ, None),
        P(DP, SEQ, None),
        P(DP),
        P(DP),
        P(DP),
        P(),
        P(),
        P(),
        P(DP, None),
        P(DP, SEQ),
        P(DP, SEQ),
        P(DP, SEQ),
        P(DP, SEQ),
        P(DP, SEQ),
    )
    out_specs = (
        P(DP, SEQ, None),
        P(DP, SEQ, None),
        P(DP, SEQ),
        P(DP, SEQ),
        P(DP, SEQ),
        P(DP, SEQ),
    )
    return jax.shard_map(local, mesh=fine, in_specs=in_specs, out_specs=out_specs, check_vma=False)
```

time: 365 us -> 160 us (0.44)
  waiting for transfers between devices: 199 us -> 49.4 us
  blocking collectives: 53 us -> 0 us
  matrix products: 21.7 us -> 0 us
  Pallas kernels: 0 us -> 16.6 us
  starting transfers between devices: 55.4 us -> 63.9 us
  other arithmetic: 8.4 us -> 4.53 us
    reduce_scatter x1 -> x0, waiting for transfers between devices: 118 us -> none  [local(): lax.psum_scatter(lax.dot_general(saved_attention, output_cotangent, (((0,...]
    all_gather x1 -> x0, blocking collectives: 53 us -> none  [local(): column_slab = lax.all_gather(sampler_weight, 'dp', axis=0, tiled=True)]
    ppermute x0 -> x8, starting transfers between devices: none -> 43.9 us  [exchange(): return lax.ppermute(value, axis, [(k, k ^ distance) for k in range(size)])]
    ppermute x0 -> x8, waiting for transfers between devices: none -> 39.6 us  [exchange(): return lax.ppermute(value, axis, [(k, k ^ distance) for k in range(size)])]
    all_to_all x3, waiting for transfers between devices: 48.3 us -> 9.73 us  [the longest x1 9.06 us: local(): lax.all_to_all(branch, 'y', split_axis=0, concat_axis=0, tiled=True)]
    all_to_all x3, starting transfers between devices: 55.3 us -> 20 us  [the longest x1 9.62 us: local(): lax.all_to_all(heads_out, SEQ, split_axis=0, concat_axis=0, tiled=True)]
    all_gather x1, waiting for transfers between devices: 33.1 us -> 0.01 us  [local(): weight = lax.all_gather(pieces, 'z', axis=0, tiled=True)]
    dot_general x11 -> x0, matrix products: 21.7 us -> none  [the longest x1 8.9 us: local(): jnp.dot(attention_flat, lax.all_gather(column_slab, 'seq', axis=1, tiled=...]
  transfers between devices with their start and end apart: 5 -> 12, of which waited for: 5 -> 9; matrix products, arithmetic and copies ran while one was open for 6% -> 2% of each run, Pallas kernels for 0% -> 8%
where the time goes in v1:
time: 160 us; the launch traced here: 158 us
  starting transfers between devices  63.9 us (40%)
  waiting for transfers between devices  49.4 us (31%)
  Pallas kernels  16.6 us (10%)
  between operations  16.6 us (10%)
  local copies, waits for them, and re-layouts  7.08 us (4%)
  other arithmetic  4.53 us (3%)
    ppermute x8, starting transfers between devices, exchange(): return lax.ppermute(value, axis, [(k, k ^ distance) for k in range(size)])  43.9 us
    ppermute x8, waiting for transfers between devices, exchange(): return lax.ppermute(value, axis, [(k, k ^ distance) for k in range(size)])  39.6 us
    pallas_call x1, Pallas kernels, attend(): pl.pallas_call(attention_kernel, out_shape=jax.ShapeDtypeStruct((16, 4, i...  9.91 us
    all_to_all x1, starting transfers between devices, local(): lax.all_to_all(heads_out, SEQ, split_axis=0, concat_axis=0, tiled=True)  9.62 us
    all_to_all x1, waiting for transfers between devices, local(): lax.all_to_all(branch, 'y', split_axis=0, concat_axis=0, tiled=True)  9.06 us
    unnamed x33, local copies, waits for them, and re-layouts  7.08 us
    all_to_all x1, starting transfers between devices, local(): lax.all_to_all(packed, SEQ, split_axis=0, concat_axis=0, tiled=True)  5.94 us
    all_to_all x1, starting transfers between devices, local(): lax.all_to_all(branch, 'y', split_axis=0, concat_axis=0, tiled=True)  4.45 us
  transfers between devices with their start and end apart: 12, of which 9 were waited for; matrix products, arithmetic and copies ran while one was open for 2% of the time, Pallas kernels for 8%

profile of v1, /device:TPU:1, one launch (start us, length us, event | category | flops | bytes accessed | tf_op | source)
XLA Modules:
  0.0 158.1 jit_solution(6836037044379214515)
XLA Ops:
  7.2 0.0 copy-start.2
  7.2 0.0 all-gather.2.cloned.1.call-start
  7.2 1.0 convert_element_type.24
  8.2 8.8 %collective-permute-start = (bf16[64,192]{1,0:T(8,128)(2,1)S(1)}, bf16[64,192]{1,0:T(8,128)(2,1)S(1)}, u32[]{:S(2)}, u32[]{:S(2)}) collective-permute-start(bf16[64,192]{1,0:T(8,128)(2,1)S(1)} %convert_element_type.24), channel_id=1, source_target_pairs={{0,1},{1,0},{2,3},{3,2},{4,5},{5,4},{6,7},{7,6},{8,9},{9,8},{10,11... | collective-permute-start | bytes 73736 | tf_op jit(solution)/shard_map/ppermute | solution.py:219
  17.0 0.8 collective-permute-done
  17.8 0.1 pad_maximum_fusion.2
  17.9 1.9 %collective-permute-start.1 = (bf16[64,384]{1,0:T(8,128)(2,1)S(1)}, bf16[64,384]{1,0:T(8,128)(2,1)S(1)}, u32[]{:S(2)}, u32[]{:S(2)}) collective-permute-start(bf16[64,384]{1,0:T(8,128)(2,1)S(1)} %pad_maximum_fusion.2), channel_id=1, source_target_pairs={{0,8},{8,0},{1,9},{9,1},{2,10},{10,2},{3,11},{11,3},{4,12},{12,4},... | collective-permute-start | bytes 147464 | tf_op jit(solution)/shard_map/ppermute | solution.py:219
  19.8 4.4 %collective-permute-done.1 = bf16[64,384]{1,0:T(8,128)(2,1)S(1)} collective-permute-done((bf16[64,384]{1,0:T(8,128)(2,1)S(1)}, bf16[64,384]{1,0:T(8,128)(2,1)S(1)}, u32[]{:S(2)}, u32[]{:S(2)}) %collective-permute-start.1) | collective-permute-done | bytes 49184 | tf_op jit(solution)/shard_map/ppermute | solution.py:219
  24.2 0.1 broadcast_select_fusion.3
  24.3 0.0 copy-start.7
  24.3 0.0 copy-start.8
  24.3 0.6 copy-done.7
  24.9 0.6 pad_maximum_fusion.1
  25.6 0.0 copy-done.8
  25.6 1.9 %collective-permute-start.2 = (bf16[64,768]{1,0:T(8,128)(2,1)}, bf16[64,768]{1,0:T(8,128)(2,1)}, u32[]{:S(2)}, u32[]{:S(2)}) collective-permute-start(bf16[64,768]{1,0:T(8,128)(2,1)} %pad_maximum_fusion.1), channel_id=1, source_target_pairs={{0,16},{16,0},{1,17},{17,1},{2,18},{18,2},{3,19},{19,3},{4,20},{20... | collective-permute-start | bytes 294920 | tf_op jit(solution)/shard_map/ppermute | solution.py:219
  27.5 1.0 copy.22.cotangent_ref
  28.5 0.0 copy-start.3
  28.5 1.2 copy-done.3
  29.7 0.5 partial.1
  30.3 1.9 %collective-permute-start.3 = (bf16[16,64,192]{2,1,0:T(8,128)(2,1)S(1)}, bf16[16,64,192]{2,1,0:T(8,128)(2,1)S(1)}, u32[]{:S(2)}, u32[]{:S(2)}) collective-permute-start(bf16[16,64,192]{2,1,0:T(8,128)(2,1)S(1)} %get-tuple-element.28), channel_id=1, source_target_pairs={{0,32},{32,0},{64,96},{96,64},{128,160},{160,128},{192,224},{224,1... | collective-permute-start | bytes 1179656 | tf_op jit(solution)/shard_map/ppermute | solution.py:219
  32.2 0.0 copy-done.2
  32.2 0.0 copy-start.6
  32.2 1.0 copy-done.6
  33.2 1.7 %pack.1 = bf16[16,3,160,128]{3,2,1,0:T(8,128)(2,1)} custom-call(bf16[3,128,2048]{2,1,0:T(8,128)(2,1)S(1)} %bitcast.48, bf16[3,32,2048]{2,1,0:T(8,128)(2,1)S(1)} %bitcast.51), custom_call_target="tpu_custom_call" | custom-call | tf_op jit(solution)/shard_map/pack/pallas_call | solution.py:53
  34.9 0.0 collective-permute-done.2
  34.9 0.9 broadcast_select_fusion.1
  35.8 0.7 pad_maximum_fusion
  36.5 7.6 %collective-permute-done.3.taken_ref = bf16[16,64,192]{2,1,0:T(8,128)(2,1)S(1)} collective-permute-done((bf16[16,64,192]{2,1,0:T(8,128)(2,1)S(1)}, bf16[16,64,192]{2,1,0:T(8,128)(2,1)S(1)}, u32[]{:S(2)}, u32[]{:S(2)}) %collective-permute-start.3) | collective-permute-done | bytes 393248 | tf_op jit(solution)/shard_map/ppermute | solution.py:219
  44.1 0.0 all-gather.2.cloned.1.call-update
  44.1 5.9 %all-to-all-start = ((bf16[16,3,160,128]{3,2,1,0:T(8,128)(2,1)}), bf16[16,3,160,128]{3,2,1,0:T(8,128)(2,1)S(1)}, u32[]{:S(2)}, u32[]{:S(2)}) async-start(bf16[16,3,160,128]{3,2,1,0:T(8,128)(2,1)} %pack.1), calls=%async_computation | async-start | bytes 3932160 | tf_op jit(solution)/shard_map/all_to_all | solution.py:275
  50.0 0.2 merge.4
  50.2 4.1 %collective-permute-start.4 = (bf16[8,64,192]{2,1,0:T(8,128)(2,1)S(1)}, bf16[8,64,192]{2,1,0:T(8,128)(2,1)S(1)}, u32[]{:S(2)}, u32[]{:S(2)}) collective-permute-start(bf16[8,64,192]{2,1,0:T(8,128)(2,1)S(1)} %get-tuple-element.31), channel_id=1, source_target_pairs={{0,64},{32,96},{64,0},{96,32},{128,192},{160,224},{192,128},{224,1... | collective-permute-start | bytes 589832 | tf_op jit(solution)/shard_map/ppermute | solution.py:219
  54.3 12.6 %collective-permute-done.4.taken_ref = bf16[8,64,192]{2,1,0:T(8,128)(2,1)S(1)} collective-permute-done((bf16[8,64,192]{2,1,0:T(8,128)(2,1)S(1)}, bf16[8,64,192]{2,1,0:T(8,128)(2,1)S(1)}, u32[]{:S(2)}, u32[]{:S(2)}) %collective-permute-start.4) | collective-permute-done | bytes 196640 | tf_op jit(solution)/shard_map/ppermute | solution.py:219
  66.9 0.1 merge.5
  67.0 4.4 %collective-permute-start.5 = (bf16[4,64,192]{2,1,0:T(8,128)(2,1)S(1)}, bf16[4,64,192]{2,1,0:T(8,128)(2,1)S(1)}, u32[]{:S(2)}, u32[]{:S(2)}) collective-permute-start(bf16[4,64,192]{2,1,0:T(8,128)(2,1)S(1)} %get-tuple-element.33), channel_id=1, source_target_pairs={{0,16},{16,0},{1,17},{17,1},{2,18},{18,2},{3,19},{19,3},{4,20},{20... | collective-permute-start | bytes 294920 | tf_op jit(solution)/shard_map/ppermute | solution.py:219
  71.4 5.1 %collective-permute-done.5.taken_ref = bf16[4,64,192]{2,1,0:T(8,128)(2,1)S(1)} collective-permute-done((bf16[4,64,192]{2,1,0:T(8,128)(2,1)S(1)}, bf16[4,64,192]{2,1,0:T(8,128)(2,1)S(1)}, u32[]{:S(2)}, u32[]{:S(2)}) %collective-permute-start.5) | collective-permute-done | bytes 98336 | tf_op jit(solution)/shard_map/ppermute | solution.py:219
  76.5 0.7 all-to-all-done.packed_ref
  77.2 9.9 %attend.1 = bf16[16,4,128,128]{3,2,1,0:T(8,128)(2,1)S(1)} custom-call(bf16[16,3,160,128]{3,2,1,0:T(8,128)(2,1)S(1)} %all-to-all-done.packed_ref), custom_call_target="tpu_custom_call" | custom-call | flops 2700000000 | bytes 4000000 | tf_op jit(solution)/shard_map/attend/pallas_call | solution.py:96
  87.1 0.0 copy-start.1
  87.1 1.3 copy-done.1
  88.5 9.6 %all-to-all-start.1 = ((bf16[16,4,128,128]{3,2,1,0:T(8,128)(2,1)}), bf16[16,4,128,128]{3,2,1,0:T(8,128)(2,1)S(1)}, u32[]{:S(2)}, u32[]{:S(2)}) async-start(bf16[16,4,128,128]{3,2,1,0:T(8,128)(2,1)} %copy-done.1), calls=%async_computation.1 | async-start | bytes 4194304 | tf_op jit(solution)/shard_map/all_to_all | solution.py:283
  99.4 0.0 copy-done.9
  99.4 0.2 select_reduce_fusion
  99.6 6.4 %collective-permute-start.6 = (bf16[2,64,192]{2,1,0:T(8,128)(2,1)S(1)}, bf16[2,64,192]{2,1,0:T(8,128)(2,1)S(1)}, u32[]{:S(2)}, u32[]{:S(2)}) collective-permute-start(bf16[2,64,192]{2,1,0:T(8,128)(2,1)S(1)} %get-tuple-element.39), channel_id=1, source_target_pairs={{0,128},{32,160},{64,192},{96,224},{128,0},{160,32},{192,64},{224,... | collective-permute-start | bytes 147464 | tf_op jit(solution)/shard_map/ppermute | solution.py:219
  106.1 7.9 %collective-permute-done.6.taken_ref = bf16[2,64,192]{2,1,0:T(8,128)(2,1)S(1)} collective-permute-done((bf16[2,64,192]{2,1,0:T(8,128)(2,1)S(1)}, bf16[2,64,192]{2,1,0:T(8,128)(2,1)S(1)}, u32[]{:S(2)}, u32[]{:S(2)}) %collective-permute-start.6) | collective-permute-done | bytes 49184 | tf_op jit(solution)/shard_map/ppermute | solution.py:219
  114.0 14.5 %collective-permute-start.7 = (bf16[1,64,192]{2,1,0:T(8,128)(2,1)S(1)}, bf16[1,64,192]{2,1,0:T(8,128)(2,1)S(1)}, u32[]{:S(2)}, u32[]{:S(2)}) collective-permute-start(bf16[1,64,192]{2,1,0:T(8,128)(2,1)S(1)} %get-tuple-element.41), channel_id=1, source_target_pairs={{0,256},{32,288},{64,320},{96,352},{128,384},{160,416},{192,448},{... | collective-permute-start | bytes 73736 | tf_op jit(solution)/shard_map/ppermute | solution.py:219
  128.4 0.0 copy-done.11
  128.4 0.1 select_reduce_fusion.1
  128.6 1.3 collective-permute-done.7
  129.8 0.0 all-to-all-done.1
  129.8 1.9 %copy-done = bf16[2048,768]{1,0:T(8,128)(2,1)S(1)} copy-done((bf16[2048,768]{1,0:T(8,128)(2,1)S(1)}, bf16[2048,768]{1,0:T(8,128)(2,1)}, u32[]{:S(2)}) %copy-start) | copy-done | bytes 3145752
  131.7 0.0 copy-start.14
  131.8 2.7 %project.1 = bf16[512,768]{1,0:T(8,128)(2,1)} custom-call(bf16[16,512,128]{2,1,0:T(8,128)(2,1)S(1)} %bitcast.47, bf16[2048,768]{1,0:T(8,128)(2,1)S(1)} %copy-done), custom_call_target="tpu_custom_call" | custom-call | flops 1600000000 | bytes 6000000 | tf_op jit(solution)/shard_map/project/pallas_call | solution.py:121
  134.5 4.4 %all-to-all-start.2 = ((bf16[4,128,768]{2,1,0:T(8,128)(2,1)}), bf16[4,128,768]{2,1,0:T(8,128)(2,1)S(1)}, u32[]{:S(2)}, u32[]{:S(2)}) async-start(bf16[4,128,768]{2,1,0:T(8,128)(2,1)} %bitcast.12), calls=%async_computation.2 | async-start | bytes 1572864 | tf_op jit(solution)/shard_map/all_to_all | solution.py:326
  139.8 0.0 copy-done.15
  139.8 0.1 fusion.9.base_ref
  139.9 0.0 copy-done.10
  139.9 0.0 copy-done.12
  139.9 0.0 copy-done.13
  139.9 0.0 copy-done.14
  139.9 0.7 multiply_add_fusion
  140.7 9.1 %all-to-all-done.2.branch_ref = bf16[4,128,768]{2,1,0:T(8,128)(2,1)S(1)} async-done(((bf16[4,128,768]{2,1,0:T(8,128)(2,1)}), bf16[4,128,768]{2,1,0:T(8,128)(2,1)S(1)}, u32[]{:S(2)}, u32[]{:S(2)}) %all-to-all-start.2) | async-done | bytes 786464 | tf_op jit(solution)/shard_map/all_to_all | solution.py:326
  149.7 0.0 copy-done.5
  149.7 1.5 finish.1
  (19 shorter events, 0.1 us)
Async XLA Ops:
  7.2 25.0 %copy-start.2 = (bf16[1,128,3,2048]{3,1,2,0:T(8,128)(2,1)S(1)}, bf16[1,128,3,2048]{3,1,2,0:T(8,128)(2,1)}, u32[]{:S(2)}) copy-start(bf16[1,128,3,2048]{3,1,2,0:T(8,128)(2,1)} %param.16) | copy-start | bytes 4718596
  7.2 122.7 %all-gather.2.cloned.1.call-start = ((), (), s32[]{:S(2)}) async-start(), calls=%async_computation.3 | async-start | bytes 3342336 | tf_op jit(solution)/shard_map/all_gather | solution.py:273
  8.2 9.6 %collective-permute-start = (bf16[64,192]{1,0:T(8,128)(2,1)S(1)}, bf16[64,192]{1,0:T(8,128)(2,1)S(1)}, u32[]{:S(2)}, u32[]{:S(2)}) collective-permute-start(bf16[64,192]{1,0:T(8,128)(2,1)S(1)} %convert_element_type.24), channel_id=1, source_target_pairs={{0,1},{1,0},{2,3},{3,2},{4,5},{5,4},{6,7},{7,6},{8,9},{9,8},{10,11... | collective-permute-start | bytes 73736 | tf_op jit(solution)/shard_map/ppermute | solution.py:219
  17.9 6.3 %collective-permute-start.1 = (bf16[64,384]{1,0:T(8,128)(2,1)S(1)}, bf16[64,384]{1,0:T(8,128)(2,1)S(1)}, u32[]{:S(2)}, u32[]{:S(2)}) collective-permute-start(bf16[64,384]{1,0:T(8,128)(2,1)S(1)} %pad_maximum_fusion.2), channel_id=1, source_target_pairs={{0,8},{8,0},{1,9},{9,1},{2,10},{10,2},{3,11},{11,3},{4,12},{12,4},... | collective-permute-start | bytes 147464 | tf_op jit(solution)/shard_map/ppermute | solution.py:219
  24.3 0.6 copy-start.7
  24.3 1.3 copy-start.8
  25.6 9.3 %collective-permute-start.2 = (bf16[64,768]{1,0:T(8,128)(2,1)}, bf16[64,768]{1,0:T(8,128)(2,1)}, u32[]{:S(2)}, u32[]{:S(2)}) collective-permute-start(bf16[64,768]{1,0:T(8,128)(2,1)} %pad_maximum_fusion.1), channel_id=1, source_target_pairs={{0,16},{16,0},{1,17},{17,1},{2,18},{18,2},{3,19},{19,3},{4,20},{20... | collective-permute-start | bytes 294920 | tf_op jit(solution)/shard_map/ppermute | solution.py:219
  28.5 1.2 copy-start.3
  30.3 13.8 %collective-permute-start.3 = (bf16[16,64,192]{2,1,0:T(8,128)(2,1)S(1)}, bf16[16,64,192]{2,1,0:T(8,128)(2,1)S(1)}, u32[]{:S(2)}, u32[]{:S(2)}) collective-permute-start(bf16[16,64,192]{2,1,0:T(8,128)(2,1)S(1)} %get-tuple-element.28), channel_id=1, source_target_pairs={{0,32},{32,0},{64,96},{96,64},{128,160},{160,128},{192,224},{224,1... | collective-permute-start | bytes 1179656 | tf_op jit(solution)/shard_map/ppermute | solution.py:219
  32.2 1.0 copy-start.6
  44.1 33.1 %all-to-all-start = ((bf16[16,3,160,128]{3,2,1,0:T(8,128)(2,1)}), bf16[16,3,160,128]{3,2,1,0:T(8,128)(2,1)S(1)}, u32[]{:S(2)}, u32[]{:S(2)}) async-start(bf16[16,3,160,128]{3,2,1,0:T(8,128)(2,1)} %pack.1), calls=%async_computation | async-start | bytes 3932160 | tf_op jit(solution)/shard_map/all_to_all | solution.py:275
  50.2 16.7 %collective-permute-start.4 = (bf16[8,64,192]{2,1,0:T(8,128)(2,1)S(1)}, bf16[8,64,192]{2,1,0:T(8,128)(2,1)S(1)}, u32[]{:S(2)}, u32[]{:S(2)}) collective-permute-start(bf16[8,64,192]{2,1,0:T(8,128)(2,1)S(1)} %get-tuple-element.31), channel_id=1, source_target_pairs={{0,64},{32,96},{64,0},{96,32},{128,192},{160,224},{192,128},{224,1... | collective-permute-start | bytes 589832 | tf_op jit(solution)/shard_map/ppermute | solution.py:219
  67.0 9.5 %collective-permute-start.5 = (bf16[4,64,192]{2,1,0:T(8,128)(2,1)S(1)}, bf16[4,64,192]{2,1,0:T(8,128)(2,1)S(1)}, u32[]{:S(2)}, u32[]{:S(2)}) collective-permute-start(bf16[4,64,192]{2,1,0:T(8,128)(2,1)S(1)} %get-tuple-element.33), channel_id=1, source_target_pairs={{0,16},{16,0},{1,17},{17,1},{2,18},{18,2},{3,19},{19,3},{4,20},{20... | collective-permute-start | bytes 294920 | tf_op jit(solution)/shard_map/ppermute | solution.py:219
  87.1 1.3 copy-start.1
  88.5 10.9 %copy-start.9 = (bf16[64,3072]{1,0:T(8,128)(2,1)S(1)}, bf16[64,3072]{1,0:T(8,128)(2,1)}, u32[]{:S(2)}) copy-start(bf16[64,3072]{1,0:T(8,128)(2,1)} %param.24) | copy-start | bytes 1179652
  88.5 40.0 %copy-start.11 = (bf16[10,3072]{1,0:T(8,128)(2,1)S(1)}, bf16[10,3072]{1,0:T(8,128)(2,1)}, u32[]{:S(2)}) copy-start(bf16[10,3072]{1,0:T(8,128)(2,1)} %param.23) | copy-start | bytes 184324
  88.5 41.4 %all-to-all-start.1 = ((bf16[16,4,128,128]{3,2,1,0:T(8,128)(2,1)}), bf16[16,4,128,128]{3,2,1,0:T(8,128)(2,1)S(1)}, u32[]{:S(2)}, u32[]{:S(2)}) async-start(bf16[16,4,128,128]{3,2,1,0:T(8,128)(2,1)} %copy-done.1), calls=%async_computation.1 | async-start | bytes 4194304 | tf_op jit(solution)/shard_map/all_to_all | solution.py:283
  99.6 14.4 %collective-permute-start.6 = (bf16[2,64,192]{2,1,0:T(8,128)(2,1)S(1)}, bf16[2,64,192]{2,1,0:T(8,128)(2,1)S(1)}, u32[]{:S(2)}, u32[]{:S(2)}) collective-permute-start(bf16[2,64,192]{2,1,0:T(8,128)(2,1)S(1)} %get-tuple-element.39), channel_id=1, source_target_pairs={{0,128},{32,160},{64,192},{96,224},{128,0},{160,32},{192,64},{224,... | collective-permute-start | bytes 147464 | tf_op jit(solution)/shard_map/ppermute | solution.py:219
  114.0 15.9 %collective-permute-start.7 = (bf16[1,64,192]{2,1,0:T(8,128)(2,1)S(1)}, bf16[1,64,192]{2,1,0:T(8,128)(2,1)S(1)}, u32[]{:S(2)}, u32[]{:S(2)}) collective-permute-start(bf16[1,64,192]{2,1,0:T(8,128)(2,1)S(1)} %get-tuple-element.41), channel_id=1, source_target_pairs={{0,256},{32,288},{64,320},{96,352},{128,384},{160,416},{192,448},{... | collective-permute-start | bytes 73736 | tf_op jit(solution)/shard_map/ppermute | solution.py:219
  129.8 1.9 %copy-start = (bf16[2048,768]{1,0:T(8,128)(2,1)S(1)}, bf16[2048,768]{1,0:T(8,128)(2,1)}, u32[]{:S(2)}) copy-start(bf16[2048,768]{1,0:T(8,128)(2,1)} %all-gather.2.cloned.1.call-done.weight_ref) | copy-start | bytes 9437188
  131.7 8.1 %copy-start.15 = (f32[1,128,64]{1,2,0:T(8,128)S(1)}, f32[1,128,64]{1,2,0:T(8,128)}, u32[]{:S(2)}) copy-start(f32[1,128,64]{1,2,0:T(8,128)} %param.19) | copy-start | bytes 98308
  131.7 8.2 %copy-start.10 = (f32[64,192]{1,0:T(8,128)S(1)}, f32[64,192]{1,0:T(8,128)}, u32[]{:S(2)}) copy-start(f32[64,192]{1,0:T(8,128)} %param.31) | copy-start | bytes 147460
  131.7 8.2 %copy-start.12 = (f32[64,192]{1,0:T(8,128)S(1)}, f32[64,192]{1,0:T(8,128)}, u32[]{:S(2)}) copy-start(f32[64,192]{1,0:T(8,128)} %param.28) | copy-start | bytes 147460
  131.7 8.2 %copy-start.13 = (f32[64,192]{1,0:T(8,128)S(1)}, f32[64,192]{1,0:T(8,128)}, u32[]{:S(2)}) copy-start(f32[64,192]{1,0:T(8,128)} %param.29) | copy-start | bytes 147460
  131.7 8.2 %copy-start.14 = (f32[64,192]{1,0:T(8,128)S(1)}, f32[64,192]{1,0:T(8,128)}, u32[]{:S(2)}) copy-start(f32[64,192]{1,0:T(8,128)} %param.30) | copy-start | bytes 147460
  134.5 15.3 %copy-start.4 = (bf16[1,128,3072]{2,1,0:T(8,128)(2,1)S(1)}, bf16[1,128,3072]{2,1,0:T(8,128)(2,1)}, u32[]{:S(2)}) copy-start(bf16[1,128,3072]{2,1,0:T(8,128)(2,1)} %param.18) | copy-start | bytes 2359300
  134.5 15.3 %copy-start.5 = (bf16[3072,64]{0,1:T(8,128)(2,1)S(1)}, bf16[3072,64]{0,1:T(8,128)(2,1)}, u32[]{:S(2)}) copy-start(bf16[3072,64]{0,1:T(8,128)(2,1)} %param.25) | copy-start | bytes 1179652
  134.5 15.2 %all-to-all-start.2 = ((bf16[4,128,768]{2,1,0:T(8,128)(2,1)}), bf16[4,128,768]{2,1,0:T(8,128)(2,1)S(1)}, u32[]{:S(2)}, u32[]{:S(2)}) async-start(bf16[4,128,768]{2,1,0:T(8,128)(2,1)} %bitcast.12), calls=%async_computation.2 | async-start | bytes 1572864 | tf_op jit(solution)/shard_map/all_to_all | solution.py:326
Sparse Core Ops, SparseCore 0:
  44.2 74.8 all-gather.1

commit v2 on v1

--- a/solution.py
+++ b/solution.py
@@ -60,7 +60,7 @@
     )(image, text)
 
 
-def attention_kernel(packed_ref, out_ref, widened_ref):
+def attention_kernel(packed_ref, out_ref, widened_ref, scores_ref):
     sources, _, tokens, width = packed_ref.shape
     image_tokens = out_ref.shape[2]
     scale = width ** (-0.5) * math.log2(math.e)
@@ -68,27 +68,32 @@
     widened_ref[:, :width] = packed_ref[:, 2].reshape(sources * tokens, width)
     widened_ref[:, width:] = jnp.ones((sources * tokens, width), jnp.bfloat16)
 
-    def step(index, carry):
-        queries = packed_ref[pl.ds(index * 2, 2), 0, :image_tokens, :]
-        queries = queries.reshape(2 * image_tokens, width)
-        scores = lax.dot_general(
-            queries, keys, (((1,), (1,)), ((), ())), preferred_element_type=jnp.float32
+    def score(index):
+        queries = packed_ref[2 * index : 2 * index + 2, 0, :image_tokens, :]
+        scores_ref[index % 2] = lax.dot_general(
+            queries.reshape(2 * image_tokens, width),
+            keys,
+            (((1,), (1,)), ((), ())),
+            preferred_element_type=jnp.float32,
         )
+
+    steps = sources // 2
+    score(0)
+    for index in range(steps):
+        if index < steps - 1:
+            score(index + 1)
+        scores = scores_ref[index % 2]
         peak = jnp.max(scores, axis=-1, keepdims=True)
         expo = jnp.exp2((scores - peak) * scale)
         mixed = jnp.dot(
             expo.astype(jnp.bfloat16), widened_ref[...], preferred_element_type=jnp.float32
         )
         result = (mixed[:, :width] / mixed[:, width:]).astype(jnp.bfloat16)
-        row = index % 4
-        half = index // 4
+        half, row = divmod(index, 4)
         for core in range(2):
             block = result[core * image_tokens : (core + 1) * image_tokens]
             for target in range(4):
                 out_ref[half * 8 + target * 2 + core, row] = block
-        return carry
-
-    lax.fori_loop(0, sources // 2, step, 0, unroll=2)
 
 
 def attend(packed, image_tokens):
@@ -98,22 +103,38 @@
         out_shape=jax.ShapeDtypeStruct((16, 4, image_tokens, HEAD_DIM), jnp.bfloat16),
         in_specs=[VMEM],
         out_specs=VMEM,
-        scratch_shapes=[pltpu.VMEM((sources * tokens, 2 * width), jnp.bfloat16)],
-        compiler_params=pltpu.CompilerParams(vmem_limit_bytes=24 * MEBI),
+        scratch_shapes=[
+            pltpu.VMEM((sources * tokens, 2 * width), jnp.bfloat16),
+            pltpu.VMEM((2, 2 * image_tokens, sources * tokens), jnp.float32),
+        ],
+        compiler_params=pltpu.CompilerParams(vmem_limit_bytes=28 * MEBI),
         cost_estimate=pl.CostEstimate(
-            flops=2700000000, bytes_accessed=4000000, transcendentals=5300000
+            flops=3000000000, bytes_accessed=4000000, transcendentals=5300000
         ),
         name="attend",
     )(packed)
 
 
-def project_kernel(heads_ref, weight_ref, out_ref, flat_ref):
+def project_kernel(heads_ref, weight_ref, out_ref, flat_ref, weight_vmem, sems):
     head_count, _, width = heads_ref.shape
+    parts = sems.shape[0]
+    rows = weight_ref.shape[0] // parts
+    copies = []
+    for part in range(parts):
+        span = pl.ds(part * rows, rows)
+        copies.append(
+            pltpu.make_async_copy(weight_ref.at[span], weight_vmem.at[span], sems.at[part])
+        )
+        copies[part].start()
     for head in range(head_count):
         flat_ref[:, head * width : (head + 1) * width] = heads_ref[head]
-    out_ref[...] = jnp.dot(
-        flat_ref[...], weight_ref[...], preferred_element_type=jnp.float32
-    ).astype(jnp.bfloat16)
+    total = None
+    for part in range(parts):
+        copies[part].wait()
+        span = slice(part * rows, (part + 1) * rows)
+        term = jnp.dot(flat_ref[:, span], weight_vmem[span], preferred_element_type=jnp.float32)
+        total = term if total is None else total + term
+    out_ref[...] = total.astype(jnp.bfloat16)
 
 
 def project(heads, weight):
@@ -121,15 +142,19 @@
     return pl.pallas_call(
         project_kernel,
         out_shape=jax.ShapeDtypeStruct((tokens, weight.shape[1]), jnp.bfloat16),
-        in_specs=[VMEM, VMEM],
+        in_specs=[VMEM, pl.BlockSpec(memory_space=pltpu.HBM)],
         out_specs=VMEM,
-        scratch_shapes=[pltpu.VMEM((tokens, head_count * width), jnp.bfloat16)],
+        scratch_shapes=[
+            pltpu.VMEM((tokens, head_count * width), jnp.bfloat16),
+            pltpu.VMEM(weight.shape, jnp.bfloat16),
+            pltpu.SemaphoreType.DMA((4,)),
+        ],
         compiler_params=pltpu.CompilerParams(vmem_limit_bytes=24 * MEBI),
         cost_estimate=pl.CostEstimate(
             flops=1600000000, bytes_accessed=6000000, transcendentals=0
         ),
         name="project",
-    )(heads, weight)
+    )(heads, pltpu.with_memory_space_constraint(weight, pltpu.HBM))
 
 
 def finish_kernel(
@@ -185,7 +210,7 @@
     partial = lax.dot_general(
         saved_ref[...],
         cotangent_ref[...],
-        (((0,), (0,)), ((), ())),
+        (((0,), (1,)), ((), ())),
         preferred_element_type=jnp.float32,
     ).astype(jnp.bfloat16)
     rows, columns = keep_ref.shape[1:]
@@ -262,17 +287,17 @@
         )
 
     order = (("z", 1, 2), ("z", 2, 2), ("xl", 1, 1), ("z", 4, 1), ("z", 8, 1))
-    keep, give = share(partial_kernel, 0, saved_attention, output_cotangent)
+    keep, give = share(partial_kernel, 0, saved_attention, output_cotangent.transpose(1, 0))
     taken = exchange(give, "z", 1)
 
-    sampler_weight = lax.optimization_barrier(average_weight.astype(jnp.bfloat16))
-    pieces = beside(sampler_weight, exchange(sampler_weight, "c", 1), "c", 1)
-    pieces = beside(pieces, exchange(pieces, "xh", 1), "xh", 1)
-    pieces = beside(pieces, exchange(pieces, "xl", 1), "xl", 0)
-    pieces, taken, packed = lax.optimization_barrier((pieces, taken, packed))
+    sampler_weight, keep = lax.optimization_barrier((average_weight.astype(jnp.bfloat16), keep))
+    pieces = lax.all_gather(sampler_weight, ("xl", "xh", "c"))
+    pieces = pieces.reshape(2, 4, own_rows, own_columns).transpose(0, 2, 1, 3)
+    pieces = pieces.reshape(2 * own_rows, 4 * own_columns)
+    pieces, taken = lax.optimization_barrier((pieces, taken))
     weight = lax.all_gather(pieces, "z", axis=0, tiled=True)
-
     arrived = lax.all_to_all(packed, SEQ, split_axis=0, concat_axis=0, tiled=True)
+
     for step in range(1, len(order)):
         keep, give = share(merge_kernel, step, keep, taken)
         if step == 3:

time: 160 us -> 148 us (0.925)
  blocking collectives: 0 us -> 17.7 us
  starting transfers between devices: 63.9 us -> 50.4 us
  waiting for transfers between devices: 49.4 us -> 37.1 us
  other arithmetic: 4.53 us -> 1.97 us
    all_gather x0 -> x1, blocking collectives: none -> 17.7 us  [local(): pieces = lax.all_gather(sampler_weight, ('xl', 'xh', 'c'))]
    ppermute x8 -> x5, waiting for transfers between devices: 39.6 us -> 28.6 us  [exchange(): return lax.ppermute(value, axis, [(k, k ^ distance) for k in range(size)])]
    ppermute x8 -> x5, starting transfers between devices: 43.9 us -> 33.7 us  [exchange(): return lax.ppermute(value, axis, [(k, k ^ distance) for k in range(size)])]
    pallas_call x1, Pallas kernels: 9.91 us -> 6.31 us  [attend(): pl.pallas_call(attention_kernel, out_shape=jax.ShapeDtypeStruct((16, 4, i...]
    unnamed x33 -> x28, local copies, waits for them, and re-layouts: 7.08 us -> 3.62 us
    reshape x0 -> x2, local copies, waits for them, and re-layouts: none -> 2.77 us  [the longest x1 1.86 us: local(): pieces = pieces.reshape(2 * own_rows, 4 * own_columns)]
    all_to_all x1, starting transfers between devices: 5.94 us -> 3.68 us  [local(): lax.all_to_all(packed, SEQ, split_axis=0, concat_axis=0, tiled=True)]
    pallas_call x1, Pallas kernels: 2.72 us -> 4.75 us  [project(): pl.pallas_call(project_kernel, out_shape=jax.ShapeDtypeStruct((tokens, we...]
  transfers between devices with their start and end apart: 12 -> 9, of which waited for: 9 -> 6; matrix products, arithmetic and copies ran while one was open for 2% -> 3% of each run, Pallas kernels for 8% -> 6%
where the time goes in v2:
time: 148 us; the launch traced here: 145 us
  starting transfers between devices  50.4 us (34%)
  waiting for transfers between devices  37.1 us (25%)
  blocking collectives  17.7 us (12%)
  between operations  16.5 us (11%)
  Pallas kernels  15.1 us (10%)
  local copies, waits for them, and re-layouts  6.39 us (4%)
  other arithmetic  1.97 us (1%)
    ppermute x5, starting transfers between devices, exchange(): return lax.ppermute(value, axis, [(k, k ^ distance) for k in range(size)])  33.7 us
    ppermute x5, waiting for transfers between devices, exchange(): return lax.ppermute(value, axis, [(k, k ^ distance) for k in range(size)])  28.6 us
    all_gather x1, blocking collectives, local(): pieces = lax.all_gather(sampler_weight, ('xl', 'xh', 'c'))  17.7 us
    all_to_all x1, starting transfers between devices, local(): lax.all_to_all(heads_out, SEQ, split_axis=0, concat_axis=0, tiled=True)  8.89 us
    all_to_all x1, waiting for transfers between devices, local(): lax.all_to_all(branch, 'y', split_axis=0, concat_axis=0, tiled=True)  8.06 us
    pallas_call x1, Pallas kernels, attend(): pl.pallas_call(attention_kernel, out_shape=jax.ShapeDtypeStruct((16, 4, i...  6.31 us
    pallas_call x1, Pallas kernels, project(): pl.pallas_call(project_kernel, out_shape=jax.ShapeDtypeStruct((tokens, we...  4.75 us
    all_to_all x1, starting transfers between devices, local(): lax.all_to_all(branch, 'y', split_axis=0, concat_axis=0, tiled=True)  4.09 us
  transfers between devices with their start and end apart: 9, of which 6 were waited for; matrix products, arithmetic and copies ran while one was open for 3% of the time, Pallas kernels for 6%

profile of v2, /device:TPU:1, one launch (start us, length us, event | category | flops | bytes accessed | tf_op | source)
XLA Modules:
  0.0 145.2 jit_solution(12600849035881295233)
XLA Ops:
  7.2 0.0 copy-start.1
  7.2 0.0 all-gather.3.cloned.1.call-start
  7.2 0.0 copy-start.2
  7.2 1.3 copy-done.2
  8.6 0.0 copy-start.6
  8.6 0.9 copy-done.6
  9.5 0.0 copy-start.5
  9.5 0.5 partial.1
  10.0 4.4 %collective-permute-start = (bf16[16,64,192]{2,1,0:T(8,128)(2,1)S(1)}, bf16[16,64,192]{2,1,0:T(8,128)(2,1)S(1)}, u32[]{:S(2)}, u32[]{:S(2)}) collective-permute-start(bf16[16,64,192]{2,1,0:T(8,128)(2,1)S(1)} %get-tuple-element.31), channel_id=1, source_target_pairs={{0,32},{32,0},{64,96},{96,64},{128,160},{160,128},{192,224},{224,1... | collective-permute-start | bytes 1179656 | tf_op jit(solution)/shard_map/ppermute | solution.py:244
  14.4 0.8 convert_element_type.24
  15.2 17.7 %all-gather = bf16[512,192]{1,0:T(8,128)(2,1)S(1)} all-gather(bf16[64,192]{1,0:T(8,128)(2,1)S(1)} %convert_element_type.24), channel_id=2, replica_groups=mesh['z'=16,'xl'=2,'xh'=2,'y'=4,'c'=2] {'xl','xh','c'}, dimensions={0}, use_global_device_ids=true | all-gather | bytes 221184 | tf_op jit(solution)/shard_map/all_gather | solution.py:294
  32.9 0.9 copy.24
  33.8 1.9 %reshape.90 = bf16[128,768]{1,0:T(8,128)(2,1)} reshape(bf16[2,64,4,192]{3,2,1,0:T(4,128)(2,1)} %bitcast.59) | data formatting | bytes 393216 | tf_op jit(solution)/shard_map/reshape | solution.py:296
  35.7 0.0 collective-permute-done.taken_ref
  35.7 0.0 all-gather.3.cloned.1.call-update
  35.7 0.0 copy-done.1
  35.7 0.0 copy-done.5
  35.7 1.7 %pack.1 = bf16[16,3,160,128]{3,2,1,0:T(8,128)(2,1)} custom-call(bf16[3,128,2048]{2,1,0:T(8,128)(2,1)S(1)} %bitcast.53, bf16[3,32,2048]{2,1,0:T(8,128)(2,1)S(1)} %bitcast.56), custom_call_target="tpu_custom_call" | custom-call | tf_op jit(solution)/shard_map/pack/pallas_call | solution.py:53
  37.4 3.7 %all-to-all-start = ((bf16[16,3,160,128]{3,2,1,0:T(8,128)(2,1)}), bf16[16,3,160,128]{3,2,1,0:T(8,128)(2,1)S(1)}, u32[]{:S(2)}, u32[]{:S(2)}) async-start(bf16[16,3,160,128]{3,2,1,0:T(8,128)(2,1)} %pack.1), calls=%async_computation | async-start | bytes 3932160 | tf_op jit(solution)/shard_map/all_to_all | solution.py:299
  41.1 0.2 merge.4
  41.2 4.9 %collective-permute-start.1 = (bf16[8,64,192]{2,1,0:T(8,128)(2,1)S(1)}, bf16[8,64,192]{2,1,0:T(8,128)(2,1)S(1)}, u32[]{:S(2)}, u32[]{:S(2)}) collective-permute-start(bf16[8,64,192]{2,1,0:T(8,128)(2,1)S(1)} %get-tuple-element.34), channel_id=1, source_target_pairs={{0,64},{32,96},{64,0},{96,32},{128,192},{160,224},{192,128},{224,1... | collective-permute-start | bytes 589832 | tf_op jit(solution)/shard_map/ppermute | solution.py:244
  46.2 15.4 %collective-permute-done.1.taken_ref = bf16[8,64,192]{2,1,0:T(8,128)(2,1)S(1)} collective-permute-done((bf16[8,64,192]{2,1,0:T(8,128)(2,1)S(1)}, bf16[8,64,192]{2,1,0:T(8,128)(2,1)S(1)}, u32[]{:S(2)}, u32[]{:S(2)}) %collective-permute-start.1) | collective-permute-done | bytes 196640 | tf_op jit(solution)/shard_map/ppermute | solution.py:244
  61.5 0.1 merge.5
  61.6 1.9 %collective-permute-start.2 = (bf16[4,64,192]{2,1,0:T(8,128)(2,1)S(1)}, bf16[4,64,192]{2,1,0:T(8,128)(2,1)S(1)}, u32[]{:S(2)}, u32[]{:S(2)}) collective-permute-start(bf16[4,64,192]{2,1,0:T(8,128)(2,1)S(1)} %get-tuple-element.36), channel_id=1, source_target_pairs={{0,16},{16,0},{1,17},{17,1},{2,18},{18,2},{3,19},{19,3},{4,20},{20... | collective-permute-start | bytes 294920 | tf_op jit(solution)/shard_map/ppermute | solution.py:244
  63.6 4.2 %collective-permute-done.2.taken_ref = bf16[4,64,192]{2,1,0:T(8,128)(2,1)S(1)} collective-permute-done((bf16[4,64,192]{2,1,0:T(8,128)(2,1)S(1)}, bf16[4,64,192]{2,1,0:T(8,128)(2,1)S(1)}, u32[]{:S(2)}, u32[]{:S(2)}) %collective-permute-start.2) | collective-permute-done | bytes 98336 | tf_op jit(solution)/shard_map/ppermute | solution.py:244
  67.8 0.5 all-to-all-done.packed_ref
  68.2 6.3 %attend.1 = bf16[16,4,128,128]{3,2,1,0:T(8,128)(2,1)S(1)} custom-call(bf16[16,3,160,128]{3,2,1,0:T(8,128)(2,1)S(1)} %all-to-all-done.packed_ref), custom_call_target="tpu_custom_call" | custom-call | flops 3000000000 | bytes 4000000 | tf_op jit(solution)/shard_map/attend/pallas_call | solution.py:101
  74.5 0.0 copy-start
  74.6 1.3 copy-done
  75.9 0.0 copy-start.7
  75.9 0.0 copy-start.9
  75.9 8.9 %all-to-all-start.1 = ((bf16[16,4,128,128]{3,2,1,0:T(8,128)(2,1)}), bf16[16,4,128,128]{3,2,1,0:T(8,128)(2,1)S(1)}, u32[]{:S(2)}, u32[]{:S(2)}) async-start(bf16[16,4,128,128]{3,2,1,0:T(8,128)(2,1)} %copy-done), calls=%async_computation.1 | async-start | bytes 4194304 | tf_op jit(solution)/shard_map/all_to_all | solution.py:308
  86.1 0.0 copy-done.7
  86.1 0.2 select_reduce_fusion
  86.3 8.6 %collective-permute-start.3 = (bf16[2,64,192]{2,1,0:T(8,128)(2,1)S(1)}, bf16[2,64,192]{2,1,0:T(8,128)(2,1)S(1)}, u32[]{:S(2)}, u32[]{:S(2)}) collective-permute-start(bf16[2,64,192]{2,1,0:T(8,128)(2,1)S(1)} %get-tuple-element.41), channel_id=1, source_target_pairs={{0,128},{32,160},{64,192},{96,224},{128,0},{160,32},{192,64},{224,... | collective-permute-start | bytes 147464 | tf_op jit(solution)/shard_map/ppermute | solution.py:244
  94.9 8.0 %collective-permute-done.3.taken_ref = bf16[2,64,192]{2,1,0:T(8,128)(2,1)S(1)} collective-permute-done((bf16[2,64,192]{2,1,0:T(8,128)(2,1)S(1)}, bf16[2,64,192]{2,1,0:T(8,128)(2,1)S(1)}, u32[]{:S(2)}, u32[]{:S(2)}) %collective-permute-start.3) | collective-permute-done | bytes 49184 | tf_op jit(solution)/shard_map/ppermute | solution.py:244
  102.9 14.0 %collective-permute-start.4 = (bf16[1,64,192]{2,1,0:T(8,128)(2,1)S(1)}, bf16[1,64,192]{2,1,0:T(8,128)(2,1)S(1)}, u32[]{:S(2)}, u32[]{:S(2)}) collective-permute-start(bf16[1,64,192]{2,1,0:T(8,128)(2,1)S(1)} %get-tuple-element.43), channel_id=1, source_target_pairs={{0,256},{32,288},{64,320},{96,352},{128,384},{160,416},{192,448},{... | collective-permute-start | bytes 73736 | tf_op jit(solution)/shard_map/ppermute | solution.py:244
  116.9 0.0 copy-done.9
  116.9 0.1 select_reduce_fusion.1
  117.0 1.1 collective-permute-done.4
  118.1 0.0 all-to-all-done.1
  118.1 0.0 all-gather.3.cloned.1.call-done.weight_ref
  118.1 0.0 copy-start.13
  118.1 0.0 copy-start.8
  118.1 0.0 copy-start.10
  118.1 0.0 copy-start.11
  118.2 0.0 copy-start.12
  118.2 4.8 %project.1 = bf16[512,768]{1,0:T(8,128)(2,1)} custom-call(bf16[16,512,128]{2,1,0:T(8,128)(2,1)S(1)} %bitcast.52, bf16[2048,768]{1,0:T(8,128)(2,1)} %all-gather.3.cloned.1.call-done.weight_ref), custom_call_target="tpu_custom_call" | custom-call | flops 1600000000 | bytes 6000000 | tf_op jit(solution)/shard_map/project/pallas_call | solution.py:142
  122.9 0.0 copy-start.3
  122.9 0.0 copy-start.4
  123.0 4.1 %all-to-all-start.2 = ((bf16[4,128,768]{2,1,0:T(8,128)(2,1)}), bf16[4,128,768]{2,1,0:T(8,128)(2,1)S(1)}, u32[]{:S(2)}, u32[]{:S(2)}) async-start(bf16[4,128,768]{2,1,0:T(8,128)(2,1)} %bitcast.15), calls=%async_computation.2 | async-start | bytes 1572864 | tf_op jit(solution)/shard_map/all_to_all | solution.py:351
  127.9 0.0 copy-done.13
  127.9 0.1 fusion.9.base_ref
  128.0 0.0 copy-done.8
  128.0 0.0 copy-done.10
  128.0 0.0 copy-done.11
  128.1 0.0 copy-done.12
  128.1 0.7 multiply_add_fusion
  128.8 8.1 %all-to-all-done.2.branch_ref = bf16[4,128,768]{2,1,0:T(8,128)(2,1)S(1)} async-done(((bf16[4,128,768]{2,1,0:T(8,128)(2,1)}), bf16[4,128,768]{2,1,0:T(8,128)(2,1)S(1)}, u32[]{:S(2)}, u32[]{:S(2)}) %all-to-all-start.2) | async-done | bytes 786464 | tf_op jit(solution)/shard_map/all_to_all | solution.py:351
  136.9 0.0 copy-done.3
  136.9 0.0 copy-done.4
  136.9 1.5 %finish.1 = (f32[64,128]{1,0:T(8,128)}, f32[64,128]{1,0:T(8,128)}) custom-call(f32[1]{0:T(128)} %bitcast.1.slope_ref, bf16[4,128,768]{2,1,0:T(8,128)(2,1)S(1)} %all-to-all-done.2.branch_ref, bf16[128,3072]{1,0:T(8,128)(2,1)S(1)} %bitcast.54, f32[1,3072]{1,0:T(1,128)S(1)} %bitcast.58, bf16[64,3072]{1,0:T(8,128)(2,1)S(1)} %bitcast.55, ...), custom_call_target="tpu_custom_call" | custom-call | tf_op jit(solution)/shard_map/finish/pallas_call | solution.py:190
  (7 shorter events, 0.1 us)
Async XLA Ops:
  7.2 28.6 %copy-start.1 = (bf16[1,128,3,2048]{3,1,2,0:T(8,128)(2,1)S(1)}, bf16[1,128,3,2048]{3,1,2,0:T(8,128)(2,1)}, u32[]{:S(2)}) copy-start(bf16[1,128,3,2048]{3,1,2,0:T(8,128)(2,1)} %param.16) | copy-start | bytes 4718596
  7.2 110.9 %all-gather.3.cloned.1.call-start = ((), (), s32[]{:S(2)}) async-start(), calls=%async_computation.3 | async-start | bytes 3342336 | tf_op jit(solution)/shard_map/all_gather | solution.py:298
  7.2 1.3 copy-start.2
  8.6 0.9 copy-start.6
  9.5 26.3 %copy-start.5 = (bf16[1,32,3,2048]{3,1,2,0:T(8,128)(2,1)S(1)}, bf16[1,32,3,2048]{3,1,2,0:T(8,128)(2,1)}, u32[]{:S(2)}) copy-start(bf16[1,32,3,2048]{3,1,2,0:T(8,128)(2,1)} %param.17) | copy-start | bytes 1179652
  10.0 25.7 %collective-permute-start = (bf16[16,64,192]{2,1,0:T(8,128)(2,1)S(1)}, bf16[16,64,192]{2,1,0:T(8,128)(2,1)S(1)}, u32[]{:S(2)}, u32[]{:S(2)}) collective-permute-start(bf16[16,64,192]{2,1,0:T(8,128)(2,1)S(1)} %get-tuple-element.31), channel_id=1, source_target_pairs={{0,32},{32,0},{64,96},{96,64},{128,160},{160,128},{192,224},{224,1... | collective-permute-start | bytes 1179656 | tf_op jit(solution)/shard_map/ppermute | solution.py:244
  37.4 30.8 %all-to-all-start = ((bf16[16,3,160,128]{3,2,1,0:T(8,128)(2,1)}), bf16[16,3,160,128]{3,2,1,0:T(8,128)(2,1)S(1)}, u32[]{:S(2)}, u32[]{:S(2)}) async-start(bf16[16,3,160,128]{3,2,1,0:T(8,128)(2,1)} %pack.1), calls=%async_computation | async-start | bytes 3932160 | tf_op jit(solution)/shard_map/all_to_all | solution.py:299
  41.2 20.3 %collective-permute-start.1 = (bf16[8,64,192]{2,1,0:T(8,128)(2,1)S(1)}, bf16[8,64,192]{2,1,0:T(8,128)(2,1)S(1)}, u32[]{:S(2)}, u32[]{:S(2)}) collective-permute-start(bf16[8,64,192]{2,1,0:T(8,128)(2,1)S(1)} %get-tuple-element.34), channel_id=1, source_target_pairs={{0,64},{32,96},{64,0},{96,32},{128,192},{160,224},{192,128},{224,1... | collective-permute-start | bytes 589832 | tf_op jit(solution)/shard_map/ppermute | solution.py:244
  61.6 6.1 %collective-permute-start.2 = (bf16[4,64,192]{2,1,0:T(8,128)(2,1)S(1)}, bf16[4,64,192]{2,1,0:T(8,128)(2,1)S(1)}, u32[]{:S(2)}, u32[]{:S(2)}) collective-permute-start(bf16[4,64,192]{2,1,0:T(8,128)(2,1)S(1)} %get-tuple-element.36), channel_id=1, source_target_pairs={{0,16},{16,0},{1,17},{17,1},{2,18},{18,2},{3,19},{19,3},{4,20},{20... | collective-permute-start | bytes 294920 | tf_op jit(solution)/shard_map/ppermute | solution.py:244
  74.5 1.4 copy-start
  75.9 10.2 %copy-start.7 = (bf16[64,3072]{1,0:T(8,128)(2,1)S(1)}, bf16[64,3072]{1,0:T(8,128)(2,1)}, u32[]{:S(2)}) copy-start(bf16[64,3072]{1,0:T(8,128)(2,1)} %param.24) | copy-start | bytes 1179652
  75.9 41.0 %copy-start.9 = (bf16[10,3072]{1,0:T(8,128)(2,1)S(1)}, bf16[10,3072]{1,0:T(8,128)(2,1)}, u32[]{:S(2)}) copy-start(bf16[10,3072]{1,0:T(8,128)(2,1)} %param.23) | copy-start | bytes 184324
  75.9 42.2 %all-to-all-start.1 = ((bf16[16,4,128,128]{3,2,1,0:T(8,128)(2,1)}), bf16[16,4,128,128]{3,2,1,0:T(8,128)(2,1)S(1)}, u32[]{:S(2)}, u32[]{:S(2)}) async-start(bf16[16,4,128,128]{3,2,1,0:T(8,128)(2,1)} %copy-done), calls=%async_computation.1 | async-start | bytes 4194304 | tf_op jit(solution)/shard_map/all_to_all | solution.py:308
  86.3 16.6 %collective-permute-start.3 = (bf16[2,64,192]{2,1,0:T(8,128)(2,1)S(1)}, bf16[2,64,192]{2,1,0:T(8,128)(2,1)S(1)}, u32[]{:S(2)}, u32[]{:S(2)}) collective-permute-start(bf16[2,64,192]{2,1,0:T(8,128)(2,1)S(1)} %get-tuple-element.41), channel_id=1, source_target_pairs={{0,128},{32,160},{64,192},{96,224},{128,0},{160,32},{192,64},{224,... | collective-permute-start | bytes 147464 | tf_op jit(solution)/shard_map/ppermute | solution.py:244
  102.9 15.2 %collective-permute-start.4 = (bf16[1,64,192]{2,1,0:T(8,128)(2,1)S(1)}, bf16[1,64,192]{2,1,0:T(8,128)(2,1)S(1)}, u32[]{:S(2)}, u32[]{:S(2)}) collective-permute-start(bf16[1,64,192]{2,1,0:T(8,128)(2,1)S(1)} %get-tuple-element.43), channel_id=1, source_target_pairs={{0,256},{32,288},{64,320},{96,352},{128,384},{160,416},{192,448},{... | collective-permute-start | bytes 73736 | tf_op jit(solution)/shard_map/ppermute | solution.py:244
  118.1 9.8 %copy-start.13 = (f32[1,128,64]{1,2,0:T(8,128)S(1)}, f32[1,128,64]{1,2,0:T(8,128)}, u32[]{:S(2)}) copy-start(f32[1,128,64]{1,2,0:T(8,128)} %param.19) | copy-start | bytes 98308
  118.1 9.9 %copy-start.8 = (f32[64,192]{1,0:T(8,128)S(1)}, f32[64,192]{1,0:T(8,128)}, u32[]{:S(2)}) copy-start(f32[64,192]{1,0:T(8,128)} %param.31) | copy-start | bytes 147460
  118.1 9.9 %copy-start.10 = (f32[64,192]{1,0:T(8,128)S(1)}, f32[64,192]{1,0:T(8,128)}, u32[]{:S(2)}) copy-start(f32[64,192]{1,0:T(8,128)} %param.28) | copy-start | bytes 147460
  118.1 9.9 %copy-start.11 = (f32[64,192]{1,0:T(8,128)S(1)}, f32[64,192]{1,0:T(8,128)}, u32[]{:S(2)}) copy-start(f32[64,192]{1,0:T(8,128)} %param.29) | copy-start | bytes 147460
  118.2 9.9 %copy-start.12 = (f32[64,192]{1,0:T(8,128)S(1)}, f32[64,192]{1,0:T(8,128)}, u32[]{:S(2)}) copy-start(f32[64,192]{1,0:T(8,128)} %param.30) | copy-start | bytes 147460
  122.9 13.9 %copy-start.3 = (bf16[1,128,3072]{2,1,0:T(8,128)(2,1)S(1)}, bf16[1,128,3072]{2,1,0:T(8,128)(2,1)}, u32[]{:S(2)}) copy-start(bf16[1,128,3072]{2,1,0:T(8,128)(2,1)} %param.18) | copy-start | bytes 2359300
  122.9 13.9 %copy-start.4 = (bf16[3072,64]{0,1:T(8,128)(2,1)S(1)}, bf16[3072,64]{0,1:T(8,128)(2,1)}, u32[]{:S(2)}) copy-start(bf16[3072,64]{0,1:T(8,128)(2,1)} %param.25) | copy-start | bytes 1179652
  123.0 13.9 %all-to-all-start.2 = ((bf16[4,128,768]{2,1,0:T(8,128)(2,1)}), bf16[4,128,768]{2,1,0:T(8,128)(2,1)S(1)}, u32[]{:S(2)}, u32[]{:S(2)}) async-start(bf16[4,128,768]{2,1,0:T(8,128)(2,1)} %bitcast.15), calls=%async_computation.2 | async-start | bytes 1572864 | tf_op jit(solution)/shard_map/all_to_all | solution.py:351
Sparse Core Ops, SparseCore 0:
  35.8 75.9 all-gather.2

commit v3 on v2

--- a/solution.py
+++ b/solution.py
@@ -291,9 +291,10 @@
     taken = exchange(give, "z", 1)
 
     sampler_weight, keep = lax.optimization_barrier((average_weight.astype(jnp.bfloat16), keep))
-    pieces = lax.all_gather(sampler_weight, ("xl", "xh", "c"))
-    pieces = pieces.reshape(2, 4, own_rows, own_columns).transpose(0, 2, 1, 3)
-    pieces = pieces.reshape(2 * own_rows, 4 * own_columns)
+    gathered = lax.all_gather(sampler_weight, ("xl", "xh", "c"))
+    pieces = jnp.concatenate(
+        [jnp.concatenate([gathered[4 * half + k] for k in range(4)], 1) for half in range(2)], 0
+    )
     pieces, taken = lax.optimization_barrier((pieces, taken))
     weight = lax.all_gather(pieces, "z", axis=0, tiled=True)
     arrived = lax.all_to_all(packed, SEQ, split_axis=0, concat_axis=0, tiled=True)

time: 148 us -> 146 us (0.986)
  local copies, waits for them, and re-layouts: 6.39 us -> 3.64 us
    reshape x2 -> x0, local copies, waits for them, and re-layouts: 2.77 us -> none  [the longest x1 1.86 us: local(): pieces = pieces.reshape(2 * own_rows, 4 * own_columns)]
  transfers between devices with their start and end apart: 9 -> 9, of which waited for: 6 -> 6; matrix products, arithmetic and copies ran while one was open for 3% -> 2% of each run, Pallas kernels for 6% -> 6%
where the time goes in v3:
time: 146 us; the launch traced here: 143 us
  starting transfers between devices  50.6 us (35%)
  waiting for transfers between devices  36.7 us (25%)
  blocking collectives  17.7 us (12%)
  between operations  16.5 us (11%)
  Pallas kernels  15.1 us (10%)
  local copies, waits for them, and re-layouts  3.64 us (2%)
  other arithmetic  2.78 us (2%)
    ppermute x5, starting transfers between devices, exchange(): return lax.ppermute(value, axis, [(k, k ^ distance) for k in range(size)])  33.7 us
    ppermute x5, waiting for transfers between devices, exchange(): return lax.ppermute(value, axis, [(k, k ^ distance) for k in range(size)])  28.4 us
    all_gather x1, blocking collectives, local(): gathered = lax.all_gather(sampler_weight, ('xl', 'xh', 'c'))  17.7 us
    all_to_all x1, starting transfers between devices, local(): lax.all_to_all(heads_out, SEQ, split_axis=0, concat_axis=0, tiled=True)  8.9 us
    all_to_all x1, waiting for transfers between devices, local(): lax.all_to_all(branch, 'y', split_axis=0, concat_axis=0, tiled=True)  7.83 us
    pallas_call x1, Pallas kernels, attend(): pl.pallas_call(attention_kernel, out_shape=jax.ShapeDtypeStruct((16, 4, i...  6.31 us
    pallas_call x1, Pallas kernels, project(): pl.pallas_call(project_kernel, out_shape=jax.ShapeDtypeStruct((tokens, we...  4.75 us
    all_to_all x1, starting transfers between devices, local(): lax.all_to_all(branch, 'y', split_axis=0, concat_axis=0, tiled=True)  4.3 us
  transfers between devices with their start and end apart: 9, of which 6 were waited for; matrix products, arithmetic and copies ran while one was open for 2% of the time, Pallas kernels for 6%

profile of v3, /device:TPU:1, one launch (start us, length us, event | category | flops | bytes accessed | tf_op | source)
XLA Modules:
  0.0 143.1 jit_solution(1755365782744991447)
XLA Ops:
  7.2 0.0 copy-start.1
  7.2 0.0 all-gather.3.cloned.1.call-start
  7.2 0.0 copy-start.2
  7.2 1.3 copy-done.2
  8.6 0.0 copy-start.6
  8.6 0.9 copy-done.6
  9.5 0.0 copy-start.5
  9.5 0.5 partial.1
  10.0 4.4 %collective-permute-start = (bf16[16,64,192]{2,1,0:T(8,128)(2,1)S(1)}, bf16[16,64,192]{2,1,0:T(8,128)(2,1)S(1)}, u32[]{:S(2)}, u32[]{:S(2)}) collective-permute-start(bf16[16,64,192]{2,1,0:T(8,128)(2,1)S(1)} %get-tuple-element.31), channel_id=1, source_target_pairs={{0,32},{32,0},{64,96},{96,64},{128,160},{160,128},{192,224},{224,1... | collective-permute-start | bytes 1179656 | tf_op jit(solution)/shard_map/ppermute | solution.py:244
  14.4 0.8 convert_element_type.24
  15.2 17.7 %all-gather = bf16[512,192]{1,0:T(8,128)(2,1)S(1)} all-gather(bf16[64,192]{1,0:T(8,128)(2,1)S(1)} %convert_element_type.24), channel_id=2, replica_groups=mesh['z'=16,'xl'=2,'xh'=2,'y'=4,'c'=2] {'xl','xh','c'}, dimensions={0}, use_global_device_ids=true | all-gather | bytes 221184 | tf_op jit(solution)/shard_map/all_gather | solution.py:294
  33.0 0.8 maximum_maximum_fusion
  33.8 0.0 collective-permute-done.taken_ref
  33.8 0.0 all-gather.3.cloned.1.call-update
  33.8 0.0 copy-done.1
  33.8 0.0 copy-done.5
  33.8 1.7 %pack.1 = bf16[16,3,160,128]{3,2,1,0:T(8,128)(2,1)} custom-call(bf16[3,128,2048]{2,1,0:T(8,128)(2,1)S(1)} %bitcast.49, bf16[3,32,2048]{2,1,0:T(8,128)(2,1)S(1)} %bitcast.52), custom_call_target="tpu_custom_call" | custom-call | tf_op jit(solution)/shard_map/pack/pallas_call | solution.py:53
  35.5 3.7 %all-to-all-start = ((bf16[16,3,160,128]{3,2,1,0:T(8,128)(2,1)}), bf16[16,3,160,128]{3,2,1,0:T(8,128)(2,1)S(1)}, u32[]{:S(2)}, u32[]{:S(2)}) async-start(bf16[16,3,160,128]{3,2,1,0:T(8,128)(2,1)} %pack.1), calls=%async_computation | async-start | bytes 3932160 | tf_op jit(solution)/shard_map/all_to_all | solution.py:300
  39.1 0.2 merge.4
  39.3 4.9 %collective-permute-start.1 = (bf16[8,64,192]{2,1,0:T(8,128)(2,1)S(1)}, bf16[8,64,192]{2,1,0:T(8,128)(2,1)S(1)}, u32[]{:S(2)}, u32[]{:S(2)}) collective-permute-start(bf16[8,64,192]{2,1,0:T(8,128)(2,1)S(1)} %get-tuple-element.34), channel_id=1, source_target_pairs={{0,64},{32,96},{64,0},{96,32},{128,192},{160,224},{192,128},{224,1... | collective-permute-start | bytes 589832 | tf_op jit(solution)/shard_map/ppermute | solution.py:244
  44.2 15.4 %collective-permute-done.1.taken_ref = bf16[8,64,192]{2,1,0:T(8,128)(2,1)S(1)} collective-permute-done((bf16[8,64,192]{2,1,0:T(8,128)(2,1)S(1)}, bf16[8,64,192]{2,1,0:T(8,128)(2,1)S(1)}, u32[]{:S(2)}, u32[]{:S(2)}) %collective-permute-start.1) | collective-permute-done | bytes 196640 | tf_op jit(solution)/shard_map/ppermute | solution.py:244
  59.6 0.1 merge.5
  59.7 1.9 %collective-permute-start.2 = (bf16[4,64,192]{2,1,0:T(8,128)(2,1)S(1)}, bf16[4,64,192]{2,1,0:T(8,128)(2,1)S(1)}, u32[]{:S(2)}, u32[]{:S(2)}) collective-permute-start(bf16[4,64,192]{2,1,0:T(8,128)(2,1)S(1)} %get-tuple-element.36), channel_id=1, source_target_pairs={{0,16},{16,0},{1,17},{17,1},{2,18},{18,2},{3,19},{19,3},{4,20},{20... | collective-permute-start | bytes 294920 | tf_op jit(solution)/shard_map/ppermute | solution.py:244
  61.6 4.2 %collective-permute-done.2.taken_ref = bf16[4,64,192]{2,1,0:T(8,128)(2,1)S(1)} collective-permute-done((bf16[4,64,192]{2,1,0:T(8,128)(2,1)S(1)}, bf16[4,64,192]{2,1,0:T(8,128)(2,1)S(1)}, u32[]{:S(2)}, u32[]{:S(2)}) %collective-permute-start.2) | collective-permute-done | bytes 98336 | tf_op jit(solution)/shard_map/ppermute | solution.py:244
  65.8 0.5 all-to-all-done.packed_ref
  66.3 6.3 %attend.1 = bf16[16,4,128,128]{3,2,1,0:T(8,128)(2,1)S(1)} custom-call(bf16[16,3,160,128]{3,2,1,0:T(8,128)(2,1)S(1)} %all-to-all-done.packed_ref), custom_call_target="tpu_custom_call" | custom-call | flops 3000000000 | bytes 4000000 | tf_op jit(solution)/shard_map/attend/pallas_call | solution.py:101
  72.6 0.0 copy-start
  72.6 1.3 copy-done
  74.0 0.0 copy-start.7
  74.0 0.0 copy-start.9
  74.0 8.9 %all-to-all-start.1 = ((bf16[16,4,128,128]{3,2,1,0:T(8,128)(2,1)}), bf16[16,4,128,128]{3,2,1,0:T(8,128)(2,1)S(1)}, u32[]{:S(2)}, u32[]{:S(2)}) async-start(bf16[16,4,128,128]{3,2,1,0:T(8,128)(2,1)} %copy-done), calls=%async_computation.1 | async-start | bytes 4194304 | tf_op jit(solution)/shard_map/all_to_all | solution.py:309
  84.2 0.0 copy-done.7
  84.2 0.2 select_reduce_fusion
  84.4 8.7 %collective-permute-start.3 = (bf16[2,64,192]{2,1,0:T(8,128)(2,1)S(1)}, bf16[2,64,192]{2,1,0:T(8,128)(2,1)S(1)}, u32[]{:S(2)}, u32[]{:S(2)}) collective-permute-start(bf16[2,64,192]{2,1,0:T(8,128)(2,1)S(1)} %get-tuple-element.41), channel_id=1, source_target_pairs={{0,128},{32,160},{64,192},{96,224},{128,0},{160,32},{192,64},{224,... | collective-permute-start | bytes 147464 | tf_op jit(solution)/shard_map/ppermute | solution.py:244
  93.1 7.9 %collective-permute-done.3.taken_ref = bf16[2,64,192]{2,1,0:T(8,128)(2,1)S(1)} collective-permute-done((bf16[2,64,192]{2,1,0:T(8,128)(2,1)S(1)}, bf16[2,64,192]{2,1,0:T(8,128)(2,1)S(1)}, u32[]{:S(2)}, u32[]{:S(2)}) %collective-permute-start.3) | collective-permute-done | bytes 49184 | tf_op jit(solution)/shard_map/ppermute | solution.py:244
  101.0 13.8 %collective-permute-start.4 = (bf16[1,64,192]{2,1,0:T(8,128)(2,1)S(1)}, bf16[1,64,192]{2,1,0:T(8,128)(2,1)S(1)}, u32[]{:S(2)}, u32[]{:S(2)}) collective-permute-start(bf16[1,64,192]{2,1,0:T(8,128)(2,1)S(1)} %get-tuple-element.43), channel_id=1, source_target_pairs={{0,256},{32,288},{64,320},{96,352},{128,384},{160,416},{192,448},{... | collective-permute-start | bytes 73736 | tf_op jit(solution)/shard_map/ppermute | solution.py:244
  114.8 0.0 copy-done.9
  114.8 0.1 select_reduce_fusion.1
  114.9 1.0 collective-permute-done.4
  116.0 0.0 all-to-all-done.1
  116.0 0.0 all-gather.3.cloned.1.call-done.weight_ref
  116.0 0.0 copy-start.13
  116.0 0.0 copy-start.8
  116.0 0.0 copy-start.10
  116.0 0.0 copy-start.11
  116.0 0.0 copy-start.12
  116.0 4.8 %project.1 = bf16[512,768]{1,0:T(8,128)(2,1)} custom-call(bf16[16,512,128]{2,1,0:T(8,128)(2,1)S(1)} %bitcast.48, bf16[2048,768]{1,0:T(8,128)(2,1)} %all-gather.3.cloned.1.call-done.weight_ref), custom_call_target="tpu_custom_call" | custom-call | flops 1600000000 | bytes 6000000 | tf_op jit(solution)/shard_map/project/pallas_call | solution.py:142
  120.8 0.0 copy-start.3
  120.8 0.0 copy-start.4
  120.8 4.3 %all-to-all-start.2 = ((bf16[4,128,768]{2,1,0:T(8,128)(2,1)}), bf16[4,128,768]{2,1,0:T(8,128)(2,1)S(1)}, u32[]{:S(2)}, u32[]{:S(2)}) async-start(bf16[4,128,768]{2,1,0:T(8,128)(2,1)} %bitcast.13), calls=%async_computation.2 | async-start | bytes 1572864 | tf_op jit(solution)/shard_map/all_to_all | solution.py:352
  126.0 0.0 copy-done.13
  126.0 0.1 fusion.9.base_ref
  126.1 0.0 copy-done.8
  126.1 0.0 copy-done.10
  126.1 0.0 copy-done.11
  126.1 0.0 copy-done.12
  126.1 0.7 multiply_add_fusion
  126.8 7.8 %all-to-all-done.2.branch_ref = bf16[4,128,768]{2,1,0:T(8,128)(2,1)S(1)} async-done(((bf16[4,128,768]{2,1,0:T(8,128)(2,1)}), bf16[4,128,768]{2,1,0:T(8,128)(2,1)S(1)}, u32[]{:S(2)}, u32[]{:S(2)}) %all-to-all-start.2) | async-done | bytes 786464 | tf_op jit(solution)/shard_map/all_to_all | solution.py:352
  134.7 0.0 copy-done.3
  134.7 0.0 copy-done.4
  134.7 1.5 %finish.1 = (f32[64,128]{1,0:T(8,128)}, f32[64,128]{1,0:T(8,128)}) custom-call(f32[1]{0:T(128)} %bitcast.1.slope_ref, bf16[4,128,768]{2,1,0:T(8,128)(2,1)S(1)} %all-to-all-done.2.branch_ref, bf16[128,3072]{1,0:T(8,128)(2,1)S(1)} %bitcast.50, f32[1,3072]{1,0:T(1,128)S(1)} %bitcast.54, bf16[64,3072]{1,0:T(8,128)(2,1)S(1)} %bitcast.51, ...), custom_call_target="tpu_custom_call" | custom-call | tf_op jit(solution)/shard_map/finish/pallas_call | solution.py:190
  (8 shorter events, 0.1 us)
Async XLA Ops:
  7.2 26.6 %copy-start.1 = (bf16[1,128,3,2048]{3,1,2,0:T(8,128)(2,1)S(1)}, bf16[1,128,3,2048]{3,1,2,0:T(8,128)(2,1)}, u32[]{:S(2)}) copy-start(bf16[1,128,3,2048]{3,1,2,0:T(8,128)(2,1)} %param.16) | copy-start | bytes 4718596
  7.2 108.8 %all-gather.3.cloned.1.call-start = ((), (), s32[]{:S(2)}) async-start(), calls=%async_computation.3 | async-start | bytes 3342336 | tf_op jit(solution)/shard_map/all_gather | solution.py:299
  7.2 1.3 copy-start.2
  8.6 0.9 copy-start.6
  9.5 24.3 %copy-start.5 = (bf16[1,32,3,2048]{3,1,2,0:T(8,128)(2,1)S(1)}, bf16[1,32,3,2048]{3,1,2,0:T(8,128)(2,1)}, u32[]{:S(2)}) copy-start(bf16[1,32,3,2048]{3,1,2,0:T(8,128)(2,1)} %param.17) | copy-start | bytes 1179652
  10.0 23.8 %collective-permute-start = (bf16[16,64,192]{2,1,0:T(8,128)(2,1)S(1)}, bf16[16,64,192]{2,1,0:T(8,128)(2,1)S(1)}, u32[]{:S(2)}, u32[]{:S(2)}) collective-permute-start(bf16[16,64,192]{2,1,0:T(8,128)(2,1)S(1)} %get-tuple-element.31), channel_id=1, source_target_pairs={{0,32},{32,0},{64,96},{96,64},{128,160},{160,128},{192,224},{224,1... | collective-permute-start | bytes 1179656 | tf_op jit(solution)/shard_map/ppermute | solution.py:244
  35.5 30.8 %all-to-all-start = ((bf16[16,3,160,128]{3,2,1,0:T(8,128)(2,1)}), bf16[16,3,160,128]{3,2,1,0:T(8,128)(2,1)S(1)}, u32[]{:S(2)}, u32[]{:S(2)}) async-start(bf16[16,3,160,128]{3,2,1,0:T(8,128)(2,1)} %pack.1), calls=%async_computation | async-start | bytes 3932160 | tf_op jit(solution)/shard_map/all_to_all | solution.py:300
  39.3 20.3 %collective-permute-start.1 = (bf16[8,64,192]{2,1,0:T(8,128)(2,1)S(1)}, bf16[8,64,192]{2,1,0:T(8,128)(2,1)S(1)}, u32[]{:S(2)}, u32[]{:S(2)}) collective-permute-start(bf16[8,64,192]{2,1,0:T(8,128)(2,1)S(1)} %get-tuple-element.34), channel_id=1, source_target_pairs={{0,64},{32,96},{64,0},{96,32},{128,192},{160,224},{192,128},{224,1... | collective-permute-start | bytes 589832 | tf_op jit(solution)/shard_map/ppermute | solution.py:244
  59.7 6.1 %collective-permute-start.2 = (bf16[4,64,192]{2,1,0:T(8,128)(2,1)S(1)}, bf16[4,64,192]{2,1,0:T(8,128)(2,1)S(1)}, u32[]{:S(2)}, u32[]{:S(2)}) collective-permute-start(bf16[4,64,192]{2,1,0:T(8,128)(2,1)S(1)} %get-tuple-element.36), channel_id=1, source_target_pairs={{0,16},{16,0},{1,17},{17,1},{2,18},{18,2},{3,19},{19,3},{4,20},{20... | collective-permute-start | bytes 294920 | tf_op jit(solution)/shard_map/ppermute | solution.py:244
  72.6 1.4 copy-start
  74.0 10.2 %copy-start.7 = (bf16[64,3072]{1,0:T(8,128)(2,1)S(1)}, bf16[64,3072]{1,0:T(8,128)(2,1)}, u32[]{:S(2)}) copy-start(bf16[64,3072]{1,0:T(8,128)(2,1)} %param.24) | copy-start | bytes 1179652
  74.0 40.9 %copy-start.9 = (bf16[10,3072]{1,0:T(8,128)(2,1)S(1)}, bf16[10,3072]{1,0:T(8,128)(2,1)}, u32[]{:S(2)}) copy-start(bf16[10,3072]{1,0:T(8,128)(2,1)} %param.23) | copy-start | bytes 184324
  74.0 42.0 %all-to-all-start.1 = ((bf16[16,4,128,128]{3,2,1,0:T(8,128)(2,1)}), bf16[16,4,128,128]{3,2,1,0:T(8,128)(2,1)S(1)}, u32[]{:S(2)}, u32[]{:S(2)}) async-start(bf16[16,4,128,128]{3,2,1,0:T(8,128)(2,1)} %copy-done), calls=%async_computation.1 | async-start | bytes 4194304 | tf_op jit(solution)/shard_map/all_to_all | solution.py:309
  84.4 16.6 %collective-permute-start.3 = (bf16[2,64,192]{2,1,0:T(8,128)(2,1)S(1)}, bf16[2,64,192]{2,1,0:T(8,128)(2,1)S(1)}, u32[]{:S(2)}, u32[]{:S(2)}) collective-permute-start(bf16[2,64,192]{2,1,0:T(8,128)(2,1)S(1)} %get-tuple-element.41), channel_id=1, source_target_pairs={{0,128},{32,160},{64,192},{96,224},{128,0},{160,32},{192,64},{224,... | collective-permute-start | bytes 147464 | tf_op jit(solution)/shard_map/ppermute | solution.py:244
  101.0 15.0 %collective-permute-start.4 = (bf16[1,64,192]{2,1,0:T(8,128)(2,1)S(1)}, bf16[1,64,192]{2,1,0:T(8,128)(2,1)S(1)}, u32[]{:S(2)}, u32[]{:S(2)}) collective-permute-start(bf16[1,64,192]{2,1,0:T(8,128)(2,1)S(1)} %get-tuple-element.43), channel_id=1, source_target_pairs={{0,256},{32,288},{64,320},{96,352},{128,384},{160,416},{192,448},{... | collective-permute-start | bytes 73736 | tf_op jit(solution)/shard_map/ppermute | solution.py:244
  116.0 10.0 %copy-start.13 = (f32[1,128,64]{1,2,0:T(8,128)S(1)}, f32[1,128,64]{1,2,0:T(8,128)}, u32[]{:S(2)}) copy-start(f32[1,128,64]{1,2,0:T(8,128)} %param.19) | copy-start | bytes 98308
  116.0 10.1 %copy-start.8 = (f32[64,192]{1,0:T(8,128)S(1)}, f32[64,192]{1,0:T(8,128)}, u32[]{:S(2)}) copy-start(f32[64,192]{1,0:T(8,128)} %param.31) | copy-start | bytes 147460
  116.0 10.1 %copy-start.10 = (f32[64,192]{1,0:T(8,128)S(1)}, f32[64,192]{1,0:T(8,128)}, u32[]{:S(2)}) copy-start(f32[64,192]{1,0:T(8,128)} %param.28) | copy-start | bytes 147460
  116.0 10.1 %copy-start.11 = (f32[64,192]{1,0:T(8,128)S(1)}, f32[64,192]{1,0:T(8,128)}, u32[]{:S(2)}) copy-start(f32[64,192]{1,0:T(8,128)} %param.29) | copy-start | bytes 147460
  116.0 10.1 %copy-start.12 = (f32[64,192]{1,0:T(8,128)S(1)}, f32[64,192]{1,0:T(8,128)}, u32[]{:S(2)}) copy-start(f32[64,192]{1,0:T(8,128)} %param.30) | copy-start | bytes 147460
  120.8 13.9 %copy-start.3 = (bf16[1,128,3072]{2,1,0:T(8,128)(2,1)S(1)}, bf16[1,128,3072]{2,1,0:T(8,128)(2,1)}, u32[]{:S(2)}) copy-start(bf16[1,128,3072]{2,1,0:T(8,128)(2,1)} %param.18) | copy-start | bytes 2359300
  120.8 13.9 %copy-start.4 = (bf16[3072,64]{0,1:T(8,128)(2,1)S(1)}, bf16[3072,64]{0,1:T(8,128)(2,1)}, u32[]{:S(2)}) copy-start(bf16[3072,64]{0,1:T(8,128)(2,1)} %param.25) | copy-start | bytes 1179652
  120.8 13.9 %all-to-all-start.2 = ((bf16[4,128,768]{2,1,0:T(8,128)(2,1)}), bf16[4,128,768]{2,1,0:T(8,128)(2,1)S(1)}, u32[]{:S(2)}, u32[]{:S(2)}) async-start(bf16[4,128,768]{2,1,0:T(8,128)(2,1)} %bitcast.13), calls=%async_computation.2 | async-start | bytes 1572864 | tf_op jit(solution)/shard_map/all_to_all | solution.py:352
Sparse Core Ops, SparseCore 0:
  33.9 76.1 all-gather.2

commit v4 on v3

--- a/solution.py
+++ b/solution.py
@@ -147,7 +147,7 @@
         scratch_shapes=[
             pltpu.VMEM((tokens, head_count * width), jnp.bfloat16),
             pltpu.VMEM(weight.shape, jnp.bfloat16),
-            pltpu.SemaphoreType.DMA((4,)),
+            pltpu.SemaphoreType.DMA((2,)),
         ],
         compiler_params=pltpu.CompilerParams(vmem_limit_bytes=24 * MEBI),
         cost_estimate=pl.CostEstimate(
@@ -272,12 +272,12 @@
 
     packed = pack(image_projected[0].transpose(1, 0, 2), text_projected[0].transpose(1, 0, 2))
 
-    def share(kernel, step, first, second):
+    def share(kernel, step, first, second, bit=None):
         axis, distance, run = order[step]
         return split_call(
             kernel,
             run,
-            axis_bit(axis, distance),
+            axis_bit(axis, distance) if bit is None else bit,
             first,
             second,
             32 >> step,
@@ -287,10 +287,15 @@
         )
 
     order = (("z", 1, 2), ("z", 2, 2), ("xl", 1, 1), ("z", 4, 1), ("z", 8, 1))
-    keep, give = share(partial_kernel, 0, saved_attention, output_cotangent.transpose(1, 0))
+    sampler_weight, first_bit = lax.optimization_barrier(
+        (average_weight.astype(jnp.bfloat16), axis_bit("z", 1))
+    )
+    keep, give = share(
+        partial_kernel, 0, saved_attention, output_cotangent.transpose(1, 0), first_bit
+    )
     taken = exchange(give, "z", 1)
 
-    sampler_weight, keep = lax.optimization_barrier((average_weight.astype(jnp.bfloat16), keep))
+    sampler_weight, keep = lax.optimization_barrier((sampler_weight, keep))
     gathered = lax.all_gather(sampler_weight, ("xl", "xh", "c"))
     pieces = jnp.concatenate(
         [jnp.concatenate([gathered[4 * half + k] for k in range(4)], 1) for half in range(2)], 0

time: 146 us -> 146 us (level)
  transfers between devices with their start and end apart: 9 -> 9, of which waited for: 6 -> 6; matrix products, arithmetic and copies ran while one was open for 2% -> 1% of each run, Pallas kernels for 6% -> 6%
where the time goes in v4:
time: 146 us; the launch traced here: 144 us
  starting transfers between devices  50.3 us (34%)
  waiting for transfers between devices  37 us (25%)
  blocking collectives  18 us (12%)
  between operations  16.5 us (11%)
  Pallas kernels  14.9 us (10%)
  local copies, waits for them, and re-layouts  3.54 us (2%)
  other arithmetic  3.5 us (2%)
    ppermute x5, starting transfers between devices, exchange(): return lax.ppermute(value, axis, [(k, k ^ distance) for k in range(size)])  33.7 us
    ppermute x5, waiting for transfers between devices, exchange(): return lax.ppermute(value, axis, [(k, k ^ distance) for k in range(size)])  28.7 us
    all_gather x1, blocking collectives, local(): gathered = lax.all_gather(sampler_weight, ('xl', 'xh', 'c'))  18 us
    all_to_all x1, starting transfers between devices, local(): lax.all_to_all(heads_out, SEQ, split_axis=0, concat_axis=0, tiled=True)  8.9 us
    all_to_all x1, waiting for transfers between devices, local(): lax.all_to_all(branch, 'y', split_axis=0, concat_axis=0, tiled=True)  7.81 us
    pallas_call x1, Pallas kernels, attend(): pl.pallas_call(attention_kernel, out_shape=jax.ShapeDtypeStruct((16, 4, i...  6.31 us
    pallas_call x1, Pallas kernels, project(): pl.pallas_call(project_kernel, out_shape=jax.ShapeDtypeStruct((tokens, we...  4.63 us
    all_to_all x1, starting transfers between devices, local(): lax.all_to_all(branch, 'y', split_axis=0, concat_axis=0, tiled=True)  4.08 us
  transfers between devices with their start and end apart: 9, of which 6 were waited for; matrix products, arithmetic and copies ran while one was open for 1% of the time, Pallas kernels for 6%

profile of v4, /device:TPU:1, one launch (start us, length us, event | category | flops | bytes accessed | tf_op | source)
XLA Modules:
  0.0 143.8 jit_solution(12133255922193105074)
XLA Ops:
  7.2 0.0 copy-start.1
  7.2 0.0 all-gather.3.cloned.1.call-start
  7.2 1.6 %convert_element_type.24 = bf16[64,192]{1,0:T(8,128)(2,1)} convert(f32[64,192]{1,0:T(8,128)} %param.31) | non-fusion elementwise | flops 12288 | bytes 73728 | tf_op jit(solution)/shard_map/convert_element_type | solution.py:291
  8.8 0.0 copy-start.2
  8.8 1.2 copy-done.2
  10.0 0.0 copy-start.6
  10.0 0.9 copy-done.6
  10.9 0.0 copy-start.5
  10.9 0.5 partial.1
  11.4 4.4 %collective-permute-start = (bf16[16,64,192]{2,1,0:T(8,128)(2,1)S(1)}, bf16[16,64,192]{2,1,0:T(8,128)(2,1)S(1)}, u32[]{:S(2)}, u32[]{:S(2)}) collective-permute-start(bf16[16,64,192]{2,1,0:T(8,128)(2,1)S(1)} %get-tuple-element.35), channel_id=1, source_target_pairs={{0,32},{32,0},{64,96},{96,64},{128,160},{160,128},{192,224},{224,1... | collective-permute-start | bytes 1179656 | tf_op jit(solution)/shard_map/ppermute | solution.py:244
  15.8 18.0 %all-gather = bf16[512,192]{1,0:T(8,128)(2,1)S(1)} all-gather(bf16[64,192]{1,0:T(8,128)(2,1)} %convert_element_type.24), channel_id=2, replica_groups=mesh['z'=16,'xl'=2,'xh'=2,'y'=4,'c'=2] {'xl','xh','c'}, dimensions={0}, use_global_device_ids=true | all-gather | bytes 221184 | tf_op jit(solution)/shard_map/all_gather | solution.py:299
  33.8 0.8 maximum_maximum_fusion
  34.6 0.0 collective-permute-done.taken_ref
  34.6 0.0 all-gather.3.cloned.1.call-update
  34.6 0.0 copy-done.1
  34.6 0.0 copy-done.5
  34.6 1.7 %pack.1 = bf16[16,3,160,128]{3,2,1,0:T(8,128)(2,1)} custom-call(bf16[3,128,2048]{2,1,0:T(8,128)(2,1)S(1)} %bitcast.49, bf16[3,32,2048]{2,1,0:T(8,128)(2,1)S(1)} %bitcast.52), custom_call_target="tpu_custom_call" | custom-call | tf_op jit(solution)/shard_map/pack/pallas_call | solution.py:53
  36.3 3.7 %all-to-all-start = ((bf16[16,3,160,128]{3,2,1,0:T(8,128)(2,1)}), bf16[16,3,160,128]{3,2,1,0:T(8,128)(2,1)S(1)}, u32[]{:S(2)}, u32[]{:S(2)}) async-start(bf16[16,3,160,128]{3,2,1,0:T(8,128)(2,1)} %pack.1), calls=%async_computation | async-start | bytes 3932160 | tf_op jit(solution)/shard_map/all_to_all | solution.py:305
  40.0 0.2 merge.4
  40.1 4.9 %collective-permute-start.1 = (bf16[8,64,192]{2,1,0:T(8,128)(2,1)S(1)}, bf16[8,64,192]{2,1,0:T(8,128)(2,1)S(1)}, u32[]{:S(2)}, u32[]{:S(2)}) collective-permute-start(bf16[8,64,192]{2,1,0:T(8,128)(2,1)S(1)} %get-tuple-element.38), channel_id=1, source_target_pairs={{0,64},{32,96},{64,0},{96,32},{128,192},{160,224},{192,128},{224,1... | collective-permute-start | bytes 589832 | tf_op jit(solution)/shard_map/ppermute | solution.py:244
  45.1 15.4 %collective-permute-done.1.taken_ref = bf16[8,64,192]{2,1,0:T(8,128)(2,1)S(1)} collective-permute-done((bf16[8,64,192]{2,1,0:T(8,128)(2,1)S(1)}, bf16[8,64,192]{2,1,0:T(8,128)(2,1)S(1)}, u32[]{:S(2)}, u32[]{:S(2)}) %collective-permute-start.1) | collective-permute-done | bytes 196640 | tf_op jit(solution)/shard_map/ppermute | solution.py:244
  60.4 0.1 merge.5
  60.5 1.9 %collective-permute-start.2 = (bf16[4,64,192]{2,1,0:T(8,128)(2,1)S(1)}, bf16[4,64,192]{2,1,0:T(8,128)(2,1)S(1)}, u32[]{:S(2)}, u32[]{:S(2)}) collective-permute-start(bf16[4,64,192]{2,1,0:T(8,128)(2,1)S(1)} %get-tuple-element.40), channel_id=1, source_target_pairs={{0,16},{16,0},{1,17},{17,1},{2,18},{18,2},{3,19},{19,3},{4,20},{20... | collective-permute-start | bytes 294920 | tf_op jit(solution)/shard_map/ppermute | solution.py:244
  62.5 4.2 %collective-permute-done.2.taken_ref = bf16[4,64,192]{2,1,0:T(8,128)(2,1)S(1)} collective-permute-done((bf16[4,64,192]{2,1,0:T(8,128)(2,1)S(1)}, bf16[4,64,192]{2,1,0:T(8,128)(2,1)S(1)}, u32[]{:S(2)}, u32[]{:S(2)}) %collective-permute-start.2) | collective-permute-done | bytes 98336 | tf_op jit(solution)/shard_map/ppermute | solution.py:244
  66.7 0.5 all-to-all-done.packed_ref
  67.1 6.3 %attend.1 = bf16[16,4,128,128]{3,2,1,0:T(8,128)(2,1)S(1)} custom-call(bf16[16,3,160,128]{3,2,1,0:T(8,128)(2,1)S(1)} %all-to-all-done.packed_ref), custom_call_target="tpu_custom_call" | custom-call | flops 3000000000 | bytes 4000000 | tf_op jit(solution)/shard_map/attend/pallas_call | solution.py:101
  73.4 0.0 copy-start
  73.4 1.3 copy-done
  74.8 0.0 copy-start.7
  74.8 0.0 copy-start.9
  74.8 8.9 %all-to-all-start.1 = ((bf16[16,4,128,128]{3,2,1,0:T(8,128)(2,1)}), bf16[16,4,128,128]{3,2,1,0:T(8,128)(2,1)S(1)}, u32[]{:S(2)}, u32[]{:S(2)}) async-start(bf16[16,4,128,128]{3,2,1,0:T(8,128)(2,1)} %copy-done), calls=%async_computation.1 | async-start | bytes 4194304 | tf_op jit(solution)/shard_map/all_to_all | solution.py:314
  85.0 0.0 copy-done.7
  85.0 0.2 select_reduce_fusion
  85.2 8.7 %collective-permute-start.3 = (bf16[2,64,192]{2,1,0:T(8,128)(2,1)S(1)}, bf16[2,64,192]{2,1,0:T(8,128)(2,1)S(1)}, u32[]{:S(2)}, u32[]{:S(2)}) collective-permute-start(bf16[2,64,192]{2,1,0:T(8,128)(2,1)S(1)} %get-tuple-element.45), channel_id=1, source_target_pairs={{0,128},{32,160},{64,192},{96,224},{128,0},{160,32},{192,64},{224,... | collective-permute-start | bytes 147464 | tf_op jit(solution)/shard_map/ppermute | solution.py:244
  93.9 7.9 %collective-permute-done.3.taken_ref = bf16[2,64,192]{2,1,0:T(8,128)(2,1)S(1)} collective-permute-done((bf16[2,64,192]{2,1,0:T(8,128)(2,1)S(1)}, bf16[2,64,192]{2,1,0:T(8,128)(2,1)S(1)}, u32[]{:S(2)}, u32[]{:S(2)}) %collective-permute-start.3) | collective-permute-done | bytes 49184 | tf_op jit(solution)/shard_map/ppermute | solution.py:244
  101.8 13.8 %collective-permute-start.4 = (bf16[1,64,192]{2,1,0:T(8,128)(2,1)S(1)}, bf16[1,64,192]{2,1,0:T(8,128)(2,1)S(1)}, u32[]{:S(2)}, u32[]{:S(2)}) collective-permute-start(bf16[1,64,192]{2,1,0:T(8,128)(2,1)S(1)} %get-tuple-element.47), channel_id=1, source_target_pairs={{0,256},{32,288},{64,320},{96,352},{128,384},{160,416},{192,448},{... | collective-permute-start | bytes 73736 | tf_op jit(solution)/shard_map/ppermute | solution.py:244
  115.6 0.0 copy-done.9
  115.6 0.1 select_reduce_fusion.1
  115.7 1.3 collective-permute-done.4
  117.0 0.0 all-to-all-done.1
  117.0 0.0 all-gather.3.cloned.1.call-done.weight_ref
  117.0 0.0 copy-start.13
  117.0 0.0 copy-start.8
  117.0 0.0 copy-start.10
  117.0 0.0 copy-start.11
  117.1 0.0 copy-start.12
  117.1 4.6 %project.1 = bf16[512,768]{1,0:T(8,128)(2,1)} custom-call(bf16[16,512,128]{2,1,0:T(8,128)(2,1)S(1)} %bitcast.48, bf16[2048,768]{1,0:T(8,128)(2,1)} %all-gather.3.cloned.1.call-done.weight_ref), custom_call_target="tpu_custom_call" | custom-call | flops 1600000000 | bytes 6000000 | tf_op jit(solution)/shard_map/project/pallas_call | solution.py:142
  121.7 0.0 copy-start.3
  121.7 0.0 copy-start.4
  121.7 4.1 %all-to-all-start.2 = ((bf16[4,128,768]{2,1,0:T(8,128)(2,1)}), bf16[4,128,768]{2,1,0:T(8,128)(2,1)S(1)}, u32[]{:S(2)}, u32[]{:S(2)}) async-start(bf16[4,128,768]{2,1,0:T(8,128)(2,1)} %bitcast.13), calls=%async_computation.2 | async-start | bytes 1572864 | tf_op jit(solution)/shard_map/all_to_all | solution.py:357
  126.7 0.0 copy-done.13
  126.7 0.1 fusion.9.base_ref
  126.8 0.0 copy-done.8
  126.8 0.0 copy-done.10
  126.8 0.0 copy-done.11
  126.8 0.0 copy-done.12
  126.8 0.7 multiply_add_fusion
  127.6 7.8 %all-to-all-done.2.branch_ref = bf16[4,128,768]{2,1,0:T(8,128)(2,1)S(1)} async-done(((bf16[4,128,768]{2,1,0:T(8,128)(2,1)}), bf16[4,128,768]{2,1,0:T(8,128)(2,1)S(1)}, u32[]{:S(2)}, u32[]{:S(2)}) %all-to-all-start.2) | async-done | bytes 786464 | tf_op jit(solution)/shard_map/all_to_all | solution.py:357
  135.4 0.0 copy-done.3
  135.4 0.0 copy-done.4
  135.4 1.5 %finish.1 = (f32[64,128]{1,0:T(8,128)}, f32[64,128]{1,0:T(8,128)}) custom-call(f32[1]{0:T(128)} %bitcast.1.slope_ref, bf16[4,128,768]{2,1,0:T(8,128)(2,1)S(1)} %all-to-all-done.2.branch_ref, bf16[128,3072]{1,0:T(8,128)(2,1)S(1)} %bitcast.50, f32[1,3072]{1,0:T(1,128)S(1)} %bitcast.54, bf16[64,3072]{1,0:T(8,128)(2,1)S(1)} %bitcast.51, ...), custom_call_target="tpu_custom_call" | custom-call | tf_op jit(solution)/shard_map/finish/pallas_call | solution.py:190
  (8 shorter events, 0.1 us)
Async XLA Ops:
  7.2 27.5 %copy-start.1 = (bf16[1,128,3,2048]{3,1,2,0:T(8,128)(2,1)S(1)}, bf16[1,128,3,2048]{3,1,2,0:T(8,128)(2,1)}, u32[]{:S(2)}) copy-start(bf16[1,128,3,2048]{3,1,2,0:T(8,128)(2,1)} %param.16) | copy-start | bytes 4718596
  7.2 109.8 %all-gather.3.cloned.1.call-start = ((), (), s32[]{:S(2)}) async-start(), calls=%async_computation.3 | async-start | bytes 3342336 | tf_op jit(solution)/shard_map/all_gather | solution.py:304
  8.8 1.2 copy-start.2
  10.0 0.9 copy-start.6
  10.9 23.7 %copy-start.5 = (bf16[1,32,3,2048]{3,1,2,0:T(8,128)(2,1)S(1)}, bf16[1,32,3,2048]{3,1,2,0:T(8,128)(2,1)}, u32[]{:S(2)}) copy-start(bf16[1,32,3,2048]{3,1,2,0:T(8,128)(2,1)} %param.17) | copy-start | bytes 1179652
  11.4 23.2 %collective-permute-start = (bf16[16,64,192]{2,1,0:T(8,128)(2,1)S(1)}, bf16[16,64,192]{2,1,0:T(8,128)(2,1)S(1)}, u32[]{:S(2)}, u32[]{:S(2)}) collective-permute-start(bf16[16,64,192]{2,1,0:T(8,128)(2,1)S(1)} %get-tuple-element.35), channel_id=1, source_target_pairs={{0,32},{32,0},{64,96},{96,64},{128,160},{160,128},{192,224},{224,1... | collective-permute-start | bytes 1179656 | tf_op jit(solution)/shard_map/ppermute | solution.py:244
  36.3 30.8 %all-to-all-start = ((bf16[16,3,160,128]{3,2,1,0:T(8,128)(2,1)}), bf16[16,3,160,128]{3,2,1,0:T(8,128)(2,1)S(1)}, u32[]{:S(2)}, u32[]{:S(2)}) async-start(bf16[16,3,160,128]{3,2,1,0:T(8,128)(2,1)} %pack.1), calls=%async_computation | async-start | bytes 3932160 | tf_op jit(solution)/shard_map/all_to_all | solution.py:305
  40.1 20.3 %collective-permute-start.1 = (bf16[8,64,192]{2,1,0:T(8,128)(2,1)S(1)}, bf16[8,64,192]{2,1,0:T(8,128)(2,1)S(1)}, u32[]{:S(2)}, u32[]{:S(2)}) collective-permute-start(bf16[8,64,192]{2,1,0:T(8,128)(2,1)S(1)} %get-tuple-element.38), channel_id=1, source_target_pairs={{0,64},{32,96},{64,0},{96,32},{128,192},{160,224},{192,128},{224,1... | collective-permute-start | bytes 589832 | tf_op jit(solution)/shard_map/ppermute | solution.py:244
  60.5 6.1 %collective-permute-start.2 = (bf16[4,64,192]{2,1,0:T(8,128)(2,1)S(1)}, bf16[4,64,192]{2,1,0:T(8,128)(2,1)S(1)}, u32[]{:S(2)}, u32[]{:S(2)}) collective-permute-start(bf16[4,64,192]{2,1,0:T(8,128)(2,1)S(1)} %get-tuple-element.40), channel_id=1, source_target_pairs={{0,16},{16,0},{1,17},{17,1},{2,18},{18,2},{3,19},{19,3},{4,20},{20... | collective-permute-start | bytes 294920 | tf_op jit(solution)/shard_map/ppermute | solution.py:244
  73.4 1.4 copy-start
  74.8 10.2 %copy-start.7 = (bf16[64,3072]{1,0:T(8,128)(2,1)S(1)}, bf16[64,3072]{1,0:T(8,128)(2,1)}, u32[]{:S(2)}) copy-start(bf16[64,3072]{1,0:T(8,128)(2,1)} %param.24) | copy-start | bytes 1179652
  74.8 40.8 %copy-start.9 = (bf16[10,3072]{1,0:T(8,128)(2,1)S(1)}, bf16[10,3072]{1,0:T(8,128)(2,1)}, u32[]{:S(2)}) copy-start(bf16[10,3072]{1,0:T(8,128)(2,1)} %param.23) | copy-start | bytes 184324
  74.8 42.2 %all-to-all-start.1 = ((bf16[16,4,128,128]{3,2,1,0:T(8,128)(2,1)}), bf16[16,4,128,128]{3,2,1,0:T(8,128)(2,1)S(1)}, u32[]{:S(2)}, u32[]{:S(2)}) async-start(bf16[16,4,128,128]{3,2,1,0:T(8,128)(2,1)} %copy-done), calls=%async_computation.1 | async-start | bytes 4194304 | tf_op jit(solution)/shard_map/all_to_all | solution.py:314
  85.2 16.6 %collective-permute-start.3 = (bf16[2,64,192]{2,1,0:T(8,128)(2,1)S(1)}, bf16[2,64,192]{2,1,0:T(8,128)(2,1)S(1)}, u32[]{:S(2)}, u32[]{:S(2)}) collective-permute-start(bf16[2,64,192]{2,1,0:T(8,128)(2,1)S(1)} %get-tuple-element.45), channel_id=1, source_target_pairs={{0,128},{32,160},{64,192},{96,224},{128,0},{160,32},{192,64},{224,... | collective-permute-start | bytes 147464 | tf_op jit(solution)/shard_map/ppermute | solution.py:244
  101.8 15.2 %collective-permute-start.4 = (bf16[1,64,192]{2,1,0:T(8,128)(2,1)S(1)}, bf16[1,64,192]{2,1,0:T(8,128)(2,1)S(1)}, u32[]{:S(2)}, u32[]{:S(2)}) collective-permute-start(bf16[1,64,192]{2,1,0:T(8,128)(2,1)S(1)} %get-tuple-element.47), channel_id=1, source_target_pairs={{0,256},{32,288},{64,320},{96,352},{128,384},{160,416},{192,448},{... | collective-permute-start | bytes 73736 | tf_op jit(solution)/shard_map/ppermute | solution.py:244
  117.0 9.7 %copy-start.13 = (f32[1,128,64]{1,2,0:T(8,128)S(1)}, f32[1,128,64]{1,2,0:T(8,128)}, u32[]{:S(2)}) copy-start(f32[1,128,64]{1,2,0:T(8,128)} %param.19) | copy-start | bytes 98308
  117.0 9.8 %copy-start.8 = (f32[64,192]{1,0:T(8,128)S(1)}, f32[64,192]{1,0:T(8,128)}, u32[]{:S(2)}) copy-start(f32[64,192]{1,0:T(8,128)} %param.31) | copy-start | bytes 147460
  117.0 9.8 %copy-start.10 = (f32[64,192]{1,0:T(8,128)S(1)}, f32[64,192]{1,0:T(8,128)}, u32[]{:S(2)}) copy-start(f32[64,192]{1,0:T(8,128)} %param.28) | copy-start | bytes 147460
  117.0 9.8 %copy-start.11 = (f32[64,192]{1,0:T(8,128)S(1)}, f32[64,192]{1,0:T(8,128)}, u32[]{:S(2)}) copy-start(f32[64,192]{1,0:T(8,128)} %param.29) | copy-start | bytes 147460
  117.1 9.8 %copy-start.12 = (f32[64,192]{1,0:T(8,128)S(1)}, f32[64,192]{1,0:T(8,128)}, u32[]{:S(2)}) copy-start(f32[64,192]{1,0:T(8,128)} %param.30) | copy-start | bytes 147460
  121.7 13.7 %copy-start.3 = (bf16[1,128,3072]{2,1,0:T(8,128)(2,1)S(1)}, bf16[1,128,3072]{2,1,0:T(8,128)(2,1)}, u32[]{:S(2)}) copy-start(bf16[1,128,3072]{2,1,0:T(8,128)(2,1)} %param.18) | copy-start | bytes 2359300
  121.7 13.7 %copy-start.4 = (bf16[3072,64]{0,1:T(8,128)(2,1)S(1)}, bf16[3072,64]{0,1:T(8,128)(2,1)}, u32[]{:S(2)}) copy-start(bf16[3072,64]{0,1:T(8,128)(2,1)} %param.25) | copy-start | bytes 1179652
  121.7 13.6 %all-to-all-start.2 = ((bf16[4,128,768]{2,1,0:T(8,128)(2,1)}), bf16[4,128,768]{2,1,0:T(8,128)(2,1)S(1)}, u32[]{:S(2)}, u32[]{:S(2)}) async-start(bf16[4,128,768]{2,1,0:T(8,128)(2,1)} %bitcast.13), calls=%async_computation.2 | async-start | bytes 1572864 | tf_op jit(solution)/shard_map/all_to_all | solution.py:357
Sparse Core Ops, SparseCore 0:
  34.7 76.1 all-gather.2
